TPU v7x, 1024 devices: a whole 8x8x8 slice. The times are simulated.
1024 devices in a mesh: dom: 64 (over z, y), inner: 16 (over x, core).
Axes of the slice: x: 8, y: 8, z: 8, core: 2. Of those that a mesh axis runs over, the one named last changes fastest.
Arguments:
- leaf_multipoles: float32 [8, 64, 524288], P(None, None, ('dom', 'inner')), may hold values from -6 to 6
- m2m_ops: float32 [8, 64, 64], replicated, may hold values from -0.25 to 0.25
- l2l_ops: float32 [8, 64, 64], replicated, may hold values from -0.75 to 0.75
- m2l_ops: float32 [189, 64, 64], replicated, may hold values from -0.0625 to 0.0625
- send_blocks: int32 [64, 16, 4, 2], P('dom', 'inner'), may hold values from 0 to 7, as said below
- send_counts: int32 [64, 16, 4], P('dom', 'inner'), may hold values from 0 to 2, as said below
- list1_src: int32 [64, 16, 8, 120], P('dom', 'inner'), may hold values from 0 to 15, as said below
- list1_pat: int32 [64, 16, 8, 120], P('dom', 'inner'), may hold values from 0 to 188
- list2_src: int32 [64, 16, 1, 8], P('dom', 'inner'), may hold values from 0 to 15
- list2_pat: int32 [64, 16, 1, 8], P('dom', 'inner'), may hold values from 0 to 188
Outputs:
- leaf_locals: float32 [8, 64, 524288], P(None, None, ('dom', 'inner'))
Inputs may be any that keep to these rules, and one draw needn't show every extreme that they name: `send_blocks`: entries are local block numbers below 8. `send_counts`: A count is zero where the destination domain d + off(w) lies outside the domains; every sender fills 2 slots for some neighbouring domain, and for every inner index some domain receives 2 blocks from each of its 4 neighbours. `list1_src`: an entry v below 8 names the device's own block v; otherwise v - 8 = w * 2 + c names slot c received from domain d + off(w), which exists, and c is below that sender's count for this device.
All inputs are finite; a program needn't handle non-finite values.
Results may differ from a plain program's by a relative error of at most 0.0003.
Values sent between devices are 32-bit elements; how exact they have to be, the bound alone decides.
No kernel may reach another device: no remote copies, remote signals or barrier semaphores. Data moves between devices by JAX's collectives and lax.ppermute only.
A program may use at most 32 MiB of HBM per device.

v0:
```python
import jax
import jax.numpy as jnp
from jax import lax
from jax.sharding import PartitionSpec as P


def shifted(block, axis, distance):
    devices = range(lax.axis_size(axis))
    route = [(i - distance, i) for i in devices if i - distance in devices]
    return lax.ppermute(block, axis, route)


def count_pairs(sources, patterns, pattern_count, column_count):
    pattern_hot = (
        patterns[:, :, None] == jnp.arange(pattern_count, dtype=jnp.int32)[None, None, :]
    ).astype(jnp.float32)
    source_hot = (
        sources[:, :, None] == jnp.arange(column_count, dtype=jnp.int32)[None, None, :]
    ).astype(jnp.float32)
    return jnp.einsum("rjp,rjs->rps", pattern_hot, source_hot, precision=lax.Precision.HIGHEST)


def apply_counts(tallies, operators, table):
    weights = jnp.einsum("rps,pck->rsck", tallies, operators, precision=lax.Precision.HIGHEST)
    return jnp.einsum("rsck,ksb->rcb", weights, table, precision=lax.Precision.HIGHEST)


def on_device(
    leaf_multipoles,
    m2m_ops,
    l2l_ops,
    m2l_ops,
    send_blocks,
    send_counts,
    list1_src,
    list1_pat,
    list2_src,
    list2_pat,
):
    precise = lax.Precision.HIGHEST
    harmonics = m2m_ops.shape[1]
    pattern_count = m2l_ops.shape[0]
    boxes_one = leaf_multipoles.shape[2]
    first_blocks = list1_src.shape[2]
    second_blocks = list2_src.shape[2]
    block_width = boxes_one // first_blocks
    window_count = send_blocks.shape[2]
    half_window = window_count // 2
    slot_count = send_blocks.shape[3]
    level1 = jnp.einsum("ock,okp->cp", m2m_ops, leaf_multipoles, precision=precise)
    grouped = level1.reshape(harmonics, boxes_one // 8, 8)
    level2 = jnp.einsum("ock,kqo->cq", m2m_ops, grouped, precision=precise)
    own_blocks = level1.reshape(harmonics, first_blocks, block_width)
    filled = (jnp.arange(slot_count, dtype=jnp.int32)[None, :] < send_counts[0, 0][:, None]).astype(
        jnp.float32
    )
    selector = (
        send_blocks[0, 0][:, :, None] == jnp.arange(first_blocks, dtype=jnp.int32)[None, None, :]
    ).astype(jnp.float32)
    selector = selector * filled[:, :, None]
    outgoing = jnp.einsum("kvb,wcv->kwcb", own_blocks, selector, precision=precise)
    arrivals = []
    for window_index in range(window_count):
        offset = (
            window_index - half_window
            if window_index < half_window
            else window_index - half_window + 1
        )
        sent = outgoing[:, window_count - 1 - window_index]
        arrivals.append(shifted(sent, "dom", -offset))
    received = jnp.stack(arrivals, axis=1)
    table_width = first_blocks + window_count * slot_count
    source_table = jnp.concatenate(
        [own_blocks, received.reshape(harmonics, window_count * slot_count, block_width)], axis=1
    )
    first_tallies = count_pairs(list1_src[0, 0], list1_pat[0, 0], pattern_count, table_width)
    far_first = apply_counts(first_tallies, m2l_ops, source_table)
    far_first = jnp.transpose(far_first, (1, 0, 2)).reshape(harmonics, boxes_one)
    domain_blocks = lax.axis_size("inner") * second_blocks
    gathered_two = lax.all_gather(level2, "inner", axis=1, tiled=True)
    domain = gathered_two.reshape(harmonics, domain_blocks, block_width)
    second_tallies = count_pairs(list2_src[0, 0], list2_pat[0, 0], pattern_count, domain_blocks)
    far_second = apply_counts(second_tallies, m2l_ops, domain)
    far_second = jnp.transpose(far_second, (1, 0, 2)).reshape(harmonics, boxes_one // 8)
    lowered = jnp.einsum("ock,kq->cqo", l2l_ops, far_second, precision=precise).reshape(
        harmonics, boxes_one
    )
    local_first = far_first + lowered
    return jnp.einsum("ock,kp->ocp", l2l_ops, local_first, precision=precise)


def solution(mesh):
    placed = (
        P(None, None, ("dom", "inner")),
        P(),
        P(),
        P(),
        P("dom", "inner", None, None),
        P("dom", "inner", None),
        P("dom", "inner", None, None),
        P("dom", "inner", None, None),
        P("dom", "inner", None, None),
        P("dom", "inner", None, None),
    )
    return jax.shard_map(
        on_device,
        mesh=mesh,
        in_specs=placed,
        out_specs=P(None, None, ("dom", "inner")),
        check_vma=False,
    )
```

profile of v0, /device:TPU:1, one launch (start us, length us, event | category | flops | bytes accessed | tf_op | source)
XLA Modules:
  0.0 109.0 jit_solution(10428216824969599864)
XLA Ops:
  0.0 0.0 copy-start
  0.0 0.0 copy-start.3
  0.0 0.0 copy-start.4
  0.0 1.2 %copy-done = f32[8,64,512]{2,1,0:T(8,128)S(1)} copy-done((f32[8,64,512]{2,1,0:T(8,128)S(1)}, f32[8,64,512]{2,1,0:T(8,128)}, u32[]{:S(2)}) %copy-start) | copy-done | bytes 1048600
  1.2 1.7 %convolution_bitcast_fusion.4 = f32[64,512]{1,0:T(8,128)S(1)} fusion(f32[8,64,64]{2,1,0:T(8,128)} %param.11, f32[8,64,512]{2,1,0:T(8,128)S(1)} %copy-done), kind=kOutput, calls=%fused_computation.9 | convolution fusion | flops 201326592 | bytes 1310720 | tf_op jit(solution)/shard_map/ock,okp->cp/dot_general | solution.py:50
  2.9 0.1 reshape.168
  3.1 0.7 compare_convert_fusion
  3.7 1.1 %convolution_bitcast_fusion.3 = f32[64,4,2,64]{3,1,0,2:T(4,128)S(1)} fusion(f32[64,8,64,1]{2,1,0,3:T(8,128)S(1)} %reshape.168, f32[4,2]{0,1:T(2,128)S(1)} %compare_convert_fusion, s32[4,2]{0,1:T(2,128)} %bitcast.95), kind=kOutput, calls=%fused_computation.8 | convolution fusion | flops 3145856 | bytes 262208 | tf_op jit(solution)/shard_map/kvb,wcv->kwcb/dot_general | solution.py:61
  4.9 0.2 fusion.29
  5.1 1.3 %collective-permute-start.3 = (f32[64,2,64]{2,0,1:T(8,128)S(1)}, f32[64,2,64]{2,0,1:T(8,128)S(1)}, u32[]{:S(2)}, u32[]{:S(2)}) collective-permute-start(f32[64,2,64]{2,0,1:T(8,128)S(1)} %bitcast.91), channel_id=1, source_target_pairs={{32,0},{48,16},{64,32},{80,48},{96,64},{112,80},{128,96},{144,112}... | collective-permute-start | bytes 98312 | tf_op jit(solution)/shard_map/ppermute | solution.py:10
  6.4 1.3 %collective-permute-start.2 = (f32[64,2,64]{2,0,1:T(8,128)S(1)}, f32[64,2,64]{2,0,1:T(8,128)S(1)}, u32[]{:S(2)}, u32[]{:S(2)}) collective-permute-start(f32[64,2,64]{2,0,1:T(8,128)S(1)} %bitcast.89), channel_id=1, source_target_pairs={{16,0},{32,16},{48,32},{64,48},{80,64},{96,80},{112,96},{128,112},... | collective-permute-start | bytes 98312 | tf_op jit(solution)/shard_map/ppermute | solution.py:10
  7.7 4.8 %collective-permute-start.1 = (f32[64,2,64]{2,0,1:T(8,128)S(1)}, f32[64,2,64]{2,0,1:T(8,128)S(1)}, u32[]{:S(2)}, u32[]{:S(2)}) collective-permute-start(f32[64,2,64]{2,0,1:T(8,128)S(1)} %bitcast.87), channel_id=1, source_target_pairs={{0,16},{16,32},{32,48},{48,64},{64,80},{80,96},{96,112},{112,128},... | collective-permute-start | bytes 98312 | tf_op jit(solution)/shard_map/ppermute | solution.py:10
  12.4 5.1 %collective-permute-start = (f32[64,2,64]{2,0,1:T(8,128)S(1)}, f32[64,2,64]{2,0,1:T(8,128)S(1)}, u32[]{:S(2)}, u32[]{:S(2)}) collective-permute-start(f32[64,2,64]{2,0,1:T(8,128)S(1)} %bitcast.85), channel_id=1, source_target_pairs={{0,32},{16,48},{32,64},{48,80},{64,96},{80,112},{96,128},{112,144}... | collective-permute-start | bytes 98312 | tf_op jit(solution)/shard_map/ppermute | solution.py:10
  17.6 0.1 copy.21
  17.7 1.3 %convolution_bitcast_fusion.6 = f32[64,64]{0,1:T(8,128)S(1)} fusion(f32[8,64,64]{2,1,0:T(8,128)} %param.11, f32[64,64,8]{0,2,1:T(8,128)S(1)} %bitcast.84), kind=kOutput, calls=%fused_computation.11 | convolution fusion | flops 25165824 | bytes 278528 | tf_op jit(solution)/shard_map/ock,kqo->cq/dot_general | solution.py:52
  19.0 29.8 %all_gather.3 = f32[64,1024]{0,1:T(8,128)S(1)} all-gather(f32[64,64]{0,1:T(8,128)S(1)} %convolution_bitcast_fusion.6), channel_id=1, replica_groups=mesh['dom'=64,'inner'=16] {'inner'}, dimensions={1}, use_global_device_ids=true | all-gather | bytes 278528 | tf_op jit(solution)/shard_map/all_gather | solution.py:80
  48.9 0.0 copy-done.3
  48.9 0.0 copy-done.4
  48.9 0.9 convolution_bitcast_fusion.1
  49.8 0.0 copy-start.5
  49.8 0.0 copy-start.6
  49.8 0.0 copy-start.1
  49.8 42.4 %fusion = f32[8,16,64,64]{3,1,2,0:T(8,128)} fusion(f32[8,189,16,1]{2,1,3,0:T(8,128)S(1)} %convolution_bitcast_fusion.1, f32[189,64,64]{0,2,1:T(8,128)} %param.13), kind=kOutput, calls=%fused_computation | convolution fusion | flops 1189085184 | bytes 5290496 | tf_op jit(solution)/shard_map/rps,pck->rsck/dot_general | solution.py:24
  92.3 0.0 copy-start.2
  92.3 0.0 copy-done.5
  92.3 0.0 copy-done.6
  92.3 0.3 convolution_bitcast_fusion.5
  92.6 0.0 copy-done.1
  92.6 5.2 %fusion.30 = f32[16,64,64]{2,0,1:T(8,128)S(1)} fusion(f32[189,16,1]{1,0,2:T(8,128)S(1)} %convolution_bitcast_fusion.5, f32[189,64,64]{0,2,1:T(8,128)S(1)} %copy-done.1), kind=kOutput, calls=%fused_computation.42 | convolution fusion | flops 148635648 | bytes 3370816 | tf_op jit(solution)/shard_map/rps,pck->rsck/dot_general | solution.py:24
  97.8 0.8 fusion.9
  98.6 0.0 copy-done.2
  98.6 0.9 convolution_bitcast_fusion.2
  99.5 0.1 reshape.158
  99.6 0.1 copy.19
  99.6 0.2 copy.42
  99.8 0.1 copy.24
  99.9 0.0 collective-permute-done.3
  99.9 0.0 collective-permute-done.2
  100.0 0.0 collective-permute-done.1
  100.0 0.0 collective-permute-done
  100.0 6.8 %fusion.4 = f32[64,8,64]{2,0,1:T(8,128)S(1)} fusion(f32[8,16,64,64]{3,1,2,0:T(8,128)} %fusion, f32[64,8,64]{2,0,1:T(8,128)S(1)} %bitcast.82, f32[64,8,64]{2,0,1:T(8,128)S(1)} %copy.19), kind=kOutput, calls=%fused_computation.6 | convolution fusion | flops 402718720 | bytes 2490368 | tf_op jit(solution)/shard_map/rsck,ksb->rcb/dot_general | solution.py:25
  106.8 0.2 copy.20
  106.9 0.1 reshape.160
  107.0 2.0 %convolution_bitcast_fusion = f32[8,64,512]{2,1,0:T(8,128)} fusion(f32[8,64,64]{2,1,0:T(8,128)S(1)} %copy-done.2, f32[64,512]{1,0:T(8,128)S(1)} %reshape.160, f32[64,512]{1,0:T(8,128)S(1)} %copy.24), kind=kOutput, calls=%fused_computation.4 | convolution fusion | flops 201359360 | bytes 1441792 | tf_op jit(solution)/shard_map/ock,kp->ocp/dot_general | solution.py:89
  (1 shorter events, 0.0 us)
Async XLA Ops:
  0.0 1.2 %copy-start = (f32[8,64,512]{2,1,0:T(8,128)S(1)}, f32[8,64,512]{2,1,0:T(8,128)}, u32[]{:S(2)}) copy-start(f32[8,64,512]{2,1,0:T(8,128)} %param.10) | copy-start | bytes 3145732
  0.0 48.9 %copy-start.3 = (s32[1,1,8,120]{3,2,1,0:T(8,128)S(1)}, s32[1,1,8,120]{3,2,1,0:T(8,128)}, u32[]{:S(2)}) copy-start(s32[1,1,8,120]{3,2,1,0:T(8,128)} %param.17) | copy-start | bytes 11524
  0.0 48.9 %copy-start.4 = (s32[1,1,8,120]{3,2,1,0:T(8,128)S(1)}, s32[1,1,8,120]{3,2,1,0:T(8,128)}, u32[]{:S(2)}) copy-start(s32[1,1,8,120]{3,2,1,0:T(8,128)} %param.16) | copy-start | bytes 11524
  5.1 94.9 %collective-permute-start.3 = (f32[64,2,64]{2,0,1:T(8,128)S(1)}, f32[64,2,64]{2,0,1:T(8,128)S(1)}, u32[]{:S(2)}, u32[]{:S(2)}) collective-permute-start(f32[64,2,64]{2,0,1:T(8,128)S(1)} %bitcast.91), channel_id=1, source_target_pairs={{32,0},{48,16},{64,32},{80,48},{96,64},{112,80},{128,96},{144,112}... | collective-permute-start | bytes 98312 | tf_op jit(solution)/shard_map/ppermute | solution.py:10
  6.4 93.6 %collective-permute-start.2 = (f32[64,2,64]{2,0,1:T(8,128)S(1)}, f32[64,2,64]{2,0,1:T(8,128)S(1)}, u32[]{:S(2)}, u32[]{:S(2)}) collective-permute-start(f32[64,2,64]{2,0,1:T(8,128)S(1)} %bitcast.89), channel_id=1, source_target_pairs={{16,0},{32,16},{48,32},{64,48},{80,64},{96,80},{112,96},{128,112},... | collective-permute-start | bytes 98312 | tf_op jit(solution)/shard_map/ppermute | solution.py:10
  7.7 92.3 %collective-permute-start.1 = (f32[64,2,64]{2,0,1:T(8,128)S(1)}, f32[64,2,64]{2,0,1:T(8,128)S(1)}, u32[]{:S(2)}, u32[]{:S(2)}) collective-permute-start(f32[64,2,64]{2,0,1:T(8,128)S(1)} %bitcast.87), channel_id=1, source_target_pairs={{0,16},{16,32},{32,48},{48,64},{64,80},{80,96},{96,112},{112,128},... | collective-permute-start | bytes 98312 | tf_op jit(solution)/shard_map/ppermute | solution.py:10
  12.4 87.5 %collective-permute-start = (f32[64,2,64]{2,0,1:T(8,128)S(1)}, f32[64,2,64]{2,0,1:T(8,128)S(1)}, u32[]{:S(2)}, u32[]{:S(2)}) collective-permute-start(f32[64,2,64]{2,0,1:T(8,128)S(1)} %bitcast.85), channel_id=1, source_target_pairs={{0,32},{16,48},{32,64},{48,80},{64,96},{80,112},{96,128},{112,144}... | collective-permute-start | bytes 98312 | tf_op jit(solution)/shard_map/ppermute | solution.py:10
  49.8 42.5 %copy-start.5 = (s32[1,1,1,8]{3,2,1,0:T(1,128)S(1)}, s32[1,1,1,8]{3,2,1,0:T(1,128)}, u32[]{:S(2)}) copy-start(s32[1,1,1,8]{3,2,1,0:T(1,128)} %param.19) | copy-start | bytes 100
  49.8 42.5 %copy-start.6 = (s32[1,1,1,8]{3,2,1,0:T(1,128)S(1)}, s32[1,1,1,8]{3,2,1,0:T(1,128)}, u32[]{:S(2)}) copy-start(s32[1,1,1,8]{3,2,1,0:T(1,128)} %param.18) | copy-start | bytes 100
  49.8 42.8 %copy-start.1 = (f32[189,64,64]{0,2,1:T(8,128)S(1)}, f32[189,64,64]{0,2,1:T(8,128)}, u32[]{:S(2)}) copy-start(f32[189,64,64]{0,2,1:T(8,128)} %param.13) | copy-start | bytes 9289732
  92.3 6.3 %copy-start.2 = (f32[8,64,64]{2,1,0:T(8,128)S(1)}, f32[8,64,64]{2,1,0:T(8,128)}, u32[]{:S(2)}) copy-start(f32[8,64,64]{2,1,0:T(8,128)} %param.12) | copy-start | bytes 393220
where the time goes:
time: 109 us
  matrix products  63.4 us (58%)
  blocking collectives  29.8 us (27%)
  starting transfers between devices  12.5 us (11%)
  local copies, waits for them, and re-layouts  2.36 us (2%)
    dot_general x2, matrix products, apply_counts(): jnp.einsum('rps,pck->rsck', tallies, operators, precision=lax.Precision.H...  47.7 us
    all_gather x1, blocking collectives, on_device(): gathered_two = lax.all_gather(level2, 'inner', axis=1, tiled=True)  29.8 us
    ppermute x4, starting transfers between devices, shifted(): return lax.ppermute(block, axis, route)  12.5 us
    dot_general x2, matrix products, apply_counts(): jnp.einsum('rsck,ksb->rcb', weights, table, precision=lax.Precision.HIGHEST)  7.55 us
  transfers between devices with their start and end apart: 4, of which 0 were waited for; matrix products, arithmetic and copies ran while one was open for 48% of the time, Pallas kernels for 0%

commit v1 on v0

v1 whole, which is shorter than its diff:
```python
import functools

import jax
import jax.numpy as jnp
from jax import lax
from jax.experimental import pallas as pl
from jax.experimental.pallas import tpu as pltpu
from jax.sharding import PartitionSpec as P

F32 = jnp.float32
BF16 = jnp.bfloat16
NT = (((1,), (1,)), ((), ()))


def split(x):
    high = x.astype(BF16)
    return high, (x - high.astype(F32)).astype(BF16)


def dot(a, b):
    return jnp.dot(a, b, preferred_element_type=F32)


def dot_nt(a, b):
    return lax.dot_general(a, b, NT, preferred_element_type=F32)


def dot3(a, b, product=dot):
    return product(a[0], b[0]) + (product(a[0], b[1]) + product(a[1], b[0]))


def lanes(shape):
    return lax.broadcasted_iota(jnp.int32, shape, len(shape) - 1)


def rows(shape):
    return lax.broadcasted_iota(jnp.int32, shape, len(shape) - 2)


def four_blocks(low, high):
    none = jnp.zeros_like(low)
    left = jnp.concatenate([low, high, none, none], axis=0)
    right = jnp.concatenate([none, none, low, high], axis=0)
    return jnp.concatenate([left, right], axis=1)


def spread(pair):
    first = lanes(pair.shape) < 64
    turned = pltpu.roll(pair, 64, 1)
    result = []
    for side in (0, 1):
        low, high = (pair, turned) if side == 0 else (turned, pair)
        low = split(jnp.where(first, low, 0.0))
        high = split(jnp.where(first, 0.0, high))
        result.append((four_blocks(low[0], high[0]), four_blocks(low[1], high[1])))
    return result


def upward_kernel(blocks_ref, counts_ref, leaf_ref, m2m_ref, level1_ref, sends_ref, level2_ref, ops, turned, grouped, twice):
    for o in range(8):
        ops[:, o * 64 : (o + 1) * 64] = m2m_ref[o]
    operators = split(ops[...])
    leaf = leaf_ref[...].reshape(512, 512)
    level1 = dot3(operators, split(leaf))
    level1_ref[...] = level1
    first = lanes((64, 128)) < 64
    for t in range(4):
        tile = level1[:, t * 128 : (t + 1) * 128]
        other = pltpu.roll(tile, 64, 1)
        twice[2 * t] = jnp.where(first, tile, other)
        twice[2 * t + 1] = jnp.where(first, other, tile)
    for w in range(4):
        count = counts_ref[0, 0, w]
        left = jnp.where(count > 0, twice[blocks_ref[0, 0, w, 0]], 0.0)
        right = jnp.where(count > 1, twice[blocks_ref[0, 0, w, 1]], 0.0)
        sends_ref[w] = jnp.where(first, left, right)
    turned[...] = jnp.concatenate([level1, level1], axis=0).T
    for o in range(8):
        grouped[:, o * 64 : (o + 1) * 64] = turned[pl.ds(o, 64, stride=8), :][:, 0:64]
    level2 = dot3(operators, split(grouped[...]), dot_nt)
    for copy in range(8):
        level2_ref[copy, :, 0:64] = level2[0:32]
        level2_ref[copy, :, 64:128] = level2[32:64]


def weights_kernel(src_ref, pat_ref, pat2_ref, m2l_ref, level1_ref, high_ref, low_ref, own_ref, second_ref, table):
    patterns = m2l_ref.shape[2]
    entries = src_ref.shape[1]
    code = src_ref[...] * 8 + rows((8, entries))
    pat = pat_ref[...]
    tally = jnp.zeros((128, patterns), F32)
    for r in range(8):
        sources = jnp.where(code[r : r + 1] == rows((128, entries)), 1.0, 0.0).astype(BF16)
        kinds = jnp.where(pat[r : r + 1] == rows((patterns, entries)), 1.0, 0.0).astype(BF16)
        tally = tally + dot_nt(sources, kinds)
    single = jnp.where(pat2_ref[...] == lanes((16, patterns)), 1.0, 0.0)
    picks = jnp.concatenate([tally, single], axis=0).astype(BF16)
    for g in range(16):
        high, low = split(jnp.concatenate([m2l_ref[16 * c + g] for c in range(4)], axis=0))
        table[g] = dot_nt(picks, high) + dot_nt(picks, low)
    for s in range(8, 16):
        high, low = split(table[:, 8 * s : 8 * s + 8, :].reshape(128, 256))
        high_ref[s - 8] = high
        low_ref[s - 8] = low
    for h in range(2):
        second_ref[h] = table[:, 128:136, 128 * h : 128 * h + 128].reshape(128, 128)
    total = jnp.zeros((128, 256), F32)
    for t in range(4):
        both = spread(level1_ref[:, t * 128 : (t + 1) * 128])
        for side in (0, 1):
            s = 2 * t + side
            total = total + dot3(split(table[:, 8 * s : 8 * s + 8, :].reshape(128, 256)), both[side])
    own_ref[...] = total


def downward_kernel(
    src2_ref, core_ref, high_ref, low_ref, own_ref, second_ref, up_ref, down_ref, level2_ref, l2l_ref, out_ref,
    total_s, wide_s
):
    core = core_ref[0]
    total = own_ref[...]
    for w, (ref, holder) in enumerate(((up_ref, 1), (up_ref, 0), (down_ref, 0), (down_ref, 1))):
        both = spread(ref[holder, core])
        for side in (0, 1):
            slot = 2 * w + side
            total = total + dot3((high_ref[slot], low_ref[slot]), both[side])
    for h in range(2):
        total_s[h] = total[:, 128 * h : 128 * h + 128]
    far = jnp.zeros((16, 256), F32)
    first = lanes((32, 128)) < 64
    for j in range(8):
        source = src2_ref[0, 0, 0, j]
        packed = level2_ref[source % 2, source // 2]
        turned = pltpu.roll(packed, 64, 1)
        low = split(jnp.where(first, jnp.concatenate([packed, turned], 0).reshape(2, 32, 128), 0.0).reshape(64, 128))
        high = split(jnp.where(first, 0.0, jnp.concatenate([turned, packed], 0).reshape(2, 32, 128)).reshape(64, 128))
        block = (four_blocks(low[0], high[0]), four_blocks(low[1], high[1]))
        operator = jnp.concatenate([second_ref[h, pl.ds(j, 16, stride=8), :] for h in range(2)], axis=1)
        far = far + dot3(split(operator), block)
    far = [far[:, 128 * h : 128 * h + 128] for h in range(2)]
    far = jnp.concatenate([part for f in far for part in (f, pltpu.roll(f, 64, 1))], axis=0)[:, 0:64]
    first = lanes((16, 128)) < 64
    local = []
    for t in range(4):
        parts = []
        for h in range(2):
            a = total_s[h, pl.ds(2 * t, 16, stride=8), :]
            b = total_s[h, pl.ds(2 * t + 1, 16, stride=8), :]
            parts.append(jnp.where(first, a, pltpu.roll(b, 64, 1)))
            parts.append(jnp.where(first, pltpu.roll(a, 64, 1), b))
        local.append(jnp.concatenate(parts, axis=0))
    local = jnp.concatenate(local, axis=1)
    operators = split(l2l_ref[...].reshape(512, 64))
    lowered = dot3(operators, split(far))
    for o in range(8):
        wide_s[:, 64 * o : 64 * o + 64] = lowered[64 * o : 64 * o + 64]
    place = 8 * (rows((512, 512)) % 64) + rows((512, 512)) // 64
    order = jnp.where(place == lanes((512, 512)), 1.0, 0.0).astype(BF16)
    wide = wide_s[...]
    head, tail = split(wide)
    local = local + (dot(head, order) + dot(tail, order))
    out_ref[...] = dot3(operators, split(local)).reshape(8, 64, 512)


def on_device(
    leaf_multipoles, m2m_ops, l2l_ops, m2l_ops, send_blocks, send_counts, list1_src, list1_pat, list2_src, list2_pat
):
    smem = pl.BlockSpec(memory_space=pltpu.SMEM)
    vmem = pl.BlockSpec(memory_space=pltpu.VMEM)
    limit = pltpu.CompilerParams(vmem_limit_bytes=40 * 1024 * 1024)
    level1, sends, level2 = pl.pallas_call(
        upward_kernel,
        out_shape=[
            jax.ShapeDtypeStruct((64, 512), F32),
            jax.ShapeDtypeStruct((4, 64, 128), F32),
            jax.ShapeDtypeStruct((8, 32, 128), F32),
        ],
        in_specs=[smem, smem, vmem, vmem],
        out_specs=[vmem] * 3,
        scratch_shapes=[
            pltpu.VMEM((64, 512), F32),
            pltpu.VMEM((512, 128), F32),
            pltpu.VMEM((64, 512), F32),
            pltpu.VMEM((8, 64, 128), F32),
        ],
        compiler_params=limit,
        name="upward",
    )(send_blocks, send_counts, leaf_multipoles, m2m_ops)

    doms, inners = lax.axis_size("dom"), lax.axis_size("inner")
    core = lax.axis_index("inner") % 2
    cores = [[2 * x, 2 * x + 1] for x in range(inners // 2)]
    chips = [[2 * x + c for x in range(inners // 2)] for c in range(2)]

    def routed(block, side):
        route = []
        for d in range(doms):
            for i in range(inners):
                to = d + side * (1 + i % 2)
                if 0 <= to < doms:
                    route.append((d * inners + i, to * inners + i))
        return lax.ppermute(block, ("dom", "inner"), route)

    def both_cores(block):
        return lax.all_gather(block, "inner", axis=0, axis_index_groups=cores)

    chip_sends = both_cores(sends)
    upper = lax.dynamic_index_in_dim(chip_sends, 2 + core, 1, keepdims=False)
    lower = lax.dynamic_index_in_dim(chip_sends, 1 - core, 1, keepdims=False)
    came_up = routed(upper, 1)
    came_down = routed(lower, -1)
    own_side = lax.all_to_all(level2, "inner", 0, 0, axis_index_groups=chips)
    all_level2 = both_cores(own_side)

    patterns = m2l_ops.shape[0]
    high, low, own, second = pl.pallas_call(
        weights_kernel,
        out_shape=[
            jax.ShapeDtypeStruct((8, 128, 256), BF16),
            jax.ShapeDtypeStruct((8, 128, 256), BF16),
            jax.ShapeDtypeStruct((128, 256), F32),
            jax.ShapeDtypeStruct((2, 128, 128), F32),
        ],
        in_specs=[vmem] * 5,
        out_specs=[vmem] * 4,
        scratch_shapes=[pltpu.VMEM((16, 144, 256), F32)],
        compiler_params=limit,
        name="weights",
    )(
        list1_src[0, 0],
        list1_pat[0, 0],
        jnp.pad(list2_pat.reshape(8, 1), ((0, 8), (0, 0)), constant_values=-1),
        jnp.transpose(m2l_ops, (1, 2, 0)),
        level1,
    )
    up = both_cores(came_up)
    down = both_cores(came_down)
    return pl.pallas_call(
        downward_kernel,
        out_shape=jax.ShapeDtypeStruct((8, 64, 512), F32),
        in_specs=[smem, smem] + [vmem] * 8,
        out_specs=vmem,
        scratch_shapes=[
            pltpu.VMEM((2, 128, 128), F32),
            pltpu.VMEM((64, 512), F32),
        ],
        compiler_params=limit,
        name="downward",
    )(list2_src, core.reshape(1), high, low, own, second, up, down, all_level2, l2l_ops)


def solution(mesh):
    placed = (
        P(None, None, ("dom", "inner")),
        P(),
        P(),
        P(),
        P("dom", "inner", None, None),
        P("dom", "inner", None),
        P("dom", "inner", None, None),
        P("dom", "inner", None, None),
        P("dom", "inner", None, None),
        P("dom", "inner", None, None),
    )
    return jax.shard_map(
        on_device,
        mesh=mesh,
        in_specs=placed,
        out_specs=P(None, None, ("dom", "inner")),
        check_vma=False,
    )
```

time: 109 us -> 48.6 us (0.45)
  matrix products: 63.4 us -> 0 us
  blocking collectives: 29.8 us -> 17.6 us
  Pallas kernels: 0 us -> 9.06 us
  local copies, waits for them, and re-layouts: 2.36 us -> 7.92 us
    dot_general x11 -> x0, matrix products: 63.4 us -> none  [the longest x2 47.7 us: apply_counts(): jnp.einsum('rps,pck->rsck', tallies, operators, precision=lax.Precision.H...]
    all_gather x1 -> x4, blocking collectives: 29.8 us -> 17.6 us  [both_cores(): return lax.all_gather(block, 'inner', axis=0, axis_index_groups=cores)]
    pallas_call x0 -> x3, Pallas kernels: none -> 9.06 us  [the longest x1 3.87 us: on_device(): pl.pallas_call(downward_kernel, out_shape=jax.ShapeDtypeStruct((8, 64, 51...]
    all_to_all x0 -> x1, starting transfers between devices: none -> 7.31 us  [on_device(): own_side = lax.all_to_all(level2, 'inner', 0, 0, axis_index_groups=chips)]
    ppermute x4 -> x2, starting transfers between devices: 12.5 us -> 6.18 us  [routed(): return lax.ppermute(block, ('dom', 'inner'), route)]
    unnamed x14 -> x17, local copies, waits for them, and re-layouts: 1.25 us -> 7.17 us
  transfers between devices with their start and end apart: 4 -> 3, of which waited for: 0 -> 0; matrix products, arithmetic and copies ran while one was open for 48% -> 2% of each run, Pallas kernels for 0% -> 6%
where the time goes in v1:
time: 48.6 us; the launch traced here: 48.2 us
  blocking collectives  17.6 us (36%)
  starting transfers between devices  13.5 us (28%)
  Pallas kernels  9.06 us (19%)
  local copies, waits for them, and re-layouts  7.92 us (16%)
    all_gather x4, blocking collectives, both_cores(): return lax.all_gather(block, 'inner', axis=0, axis_index_groups=cores)  17.6 us
    all_to_all x1, starting transfers between devices, on_device(): own_side = lax.all_to_all(level2, 'inner', 0, 0, axis_index_groups=chips)  7.31 us
    unnamed x17, local copies, waits for them, and re-layouts  7.17 us
    ppermute x2, starting transfers between devices, routed(): return lax.ppermute(block, ('dom', 'inner'), route)  6.18 us
    pallas_call x1, Pallas kernels, on_device(): pl.pallas_call(downward_kernel, out_shape=jax.ShapeDtypeStruct((8, 64, 51...  3.87 us
    pallas_call x1, Pallas kernels, on_device(): pl.pallas_call(weights_kernel, out_shape=[jax.ShapeDtypeStruct((8, 128, 2...  3.04 us
    pallas_call x1, Pallas kernels, on_device(): pl.pallas_call(upward_kernel, out_shape=[jax.ShapeDtypeStruct((64, 512),...  2.15 us
  transfers between devices with their start and end apart: 3, of which 0 were waited for; matrix products, arithmetic and copies ran while one was open for 2% of the time, Pallas kernels for 6%

profile of v1, /device:TPU:1, one launch (start us, length us, event | category | flops | bytes accessed | tf_op | source)
XLA Modules:
  0.0 48.2 jit_solution(17662871932104380214)
XLA Ops:
  0.0 0.0 copy-start.7
  0.0 0.8 %copy.14.blocks_ref = s32[1,1,4,2]{3,2,1,0:T(4,128)S(1)} copy(s32[1,1,4,2]{2,3,1,0:T(2,128)} %param.14) | data formatting | bytes 64 | tf_op args[4]
  0.8 0.0 copy-start.1
  0.8 1.2 %copy-done.1 = f32[8,64,512]{2,1,0:T(8,128)S(1)} copy-done((f32[8,64,512]{2,1,0:T(8,128)S(1)}, f32[8,64,512]{2,1,0:T(8,128)}, u32[]{:S(2)}) %copy-start.1) | copy-done | bytes 1048600
  2.0 0.0 copy-start.2
  2.0 0.9 %copy-done.2 = f32[8,64,64]{2,1,0:T(8,128)S(1)} copy-done((f32[8,64,64]{2,1,0:T(8,128)S(1)}, f32[8,64,64]{2,1,0:T(8,128)}, u32[]{:S(2)}) %copy-start.2) | copy-done | bytes 131096
  3.0 0.0 copy-start.6
  3.0 0.7 %copy-done.6 = s32[1,1,4]{2,1,0:T(1,128)S(1)} copy-done((s32[1,1,4]{2,1,0:T(1,128)S(1)}, s32[1,1,4]{2,1,0:T(1,128)}, u32[]{:S(2)}) %copy-start.6) | copy-done | bytes 40
  3.6 0.0 copy-start.3
  3.6 2.2 %upward.1 = (f32[64,512]{1,0:T(8,128)S(1)}, f32[4,64,128]{2,1,0:T(8,128)S(1)}, f32[8,32,128]{2,1,0:T(8,128)}) custom-call(s32[1,1,4,2]{3,2,1,0:T(4,128)S(1)} %copy.14.blocks_ref, s32[1,1,4]{2,1,0:T(1,128)S(1)} %copy-done.6, f32[8,64,512]{2,1,0:T(8,128)S(1)} %copy-done.1, f32[8,64,64]{2,1,0:T(8,128)S(1)} %copy-done.2), custom_call_target="tpu_custom_call" | custom-call | tf_op jit(solution)/shard_map/upward/pallas_call | solution.py:171
  5.8 7.3 %all-to-all-start = ((f32[8,32,128]{2,1,0:T(8,128)}), f32[8,32,128]{2,1,0:T(8,128)S(1)}, u32[]{:S(2)}, u32[]{:S(2)}) async-start(f32[8,32,128]{2,1,0:T(8,128)} %get-tuple-element.18), calls=%async_computation | async-start | bytes 262144 | tf_op jit(solution)/shard_map/all_to_all | solution.py:212
  13.1 11.9 %all-gather = f32[8,64,128]{2,1,0:T(8,128)S(1)} all-gather(f32[4,64,128]{2,1,0:T(8,128)S(1)} %get-tuple-element.17), channel_id=2, replica_groups={{0,1},{2,3},{4,5},{6,7},{8,9},{10,11},{12,13},{14,15},{16,17},{18,19},{..., dimensions={0}, use_global_device_ids=true | all-gather | bytes 393216 | tf_op jit(solution)/shard_map/all_gather | solution.py:205
  25.0 1.3 %collective-permute-start.1 = (f32[2,64,128]{2,1,0:T(8,128)S(1)}, f32[2,64,128]{2,1,0:T(8,128)S(1)}, u32[]{:S(2)}, u32[]{:S(2)}) collective-permute-start(f32[2,64,128]{2,1,0:T(8,128)S(1)} %get-tuple-element.19), channel_id=1, source_target_pairs={{16,0},{18,2},{20,4},{22,6},{24,8},{26,10},{28,12},{30,14},{32,16}... | collective-permute-start | bytes 196616 | tf_op jit(solution)/shard_map/ppermute | solution.py:202
  26.3 4.9 %collective-permute-start = (f32[2,64,128]{2,1,0:T(8,128)S(1)}, f32[2,64,128]{2,1,0:T(8,128)S(1)}, u32[]{:S(2)}, u32[]{:S(2)}) collective-permute-start(f32[2,64,128]{2,1,0:T(8,128)S(1)} %get-tuple-element.20), channel_id=1, source_target_pairs={{0,16},{1,33},{2,18},{3,35},{4,20},{5,37},{6,22},{7,39},{8,24},{9,... | collective-permute-start | bytes 196616 | tf_op jit(solution)/shard_map/ppermute | solution.py:202
  31.2 0.7 %copy.13 = s32[8,1]{1,0:T(8,128)S(1)} copy(s32[8,1]{0,1:T(1,128)} %bitcast.20) | data formatting | bytes 64 | tf_op jit(solution)/shard_map/reshape | solution.py:232
  31.9 0.0 copy-start
  31.9 2.2 %copy-done = f32[189,64,64]{0,2,1:T(8,128)S(1)} copy-done((f32[189,64,64]{0,2,1:T(8,128)S(1)}, f32[189,64,64]{0,2,1:T(8,128)}, u32[]{:S(2)}) %copy-start) | copy-done | bytes 3096600
  34.1 0.0 copy-start.4
  34.1 0.7 %copy-done.4 = s32[1,1,8,120]{3,2,1,0:T(8,128)S(1)} copy-done((s32[1,1,8,120]{3,2,1,0:T(8,128)S(1)}, s32[1,1,8,120]{3,2,1,0:T(8,128)}, u32[]{:S(2)}) %copy-start.4) | copy-done | bytes 3864
  34.8 0.0 copy-start.5
  34.8 0.7 %copy-done.5 = s32[1,1,8,120]{3,2,1,0:T(8,128)S(1)} copy-done((s32[1,1,8,120]{3,2,1,0:T(8,128)S(1)}, s32[1,1,8,120]{3,2,1,0:T(8,128)}, u32[]{:S(2)}) %copy-start.5) | copy-done | bytes 3864
  35.5 3.0 %weights.1 = (bf16[8,128,256]{2,1,0:T(8,128)(2,1)S(1)}, bf16[8,128,256]{2,1,0:T(8,128)(2,1)S(1)}, f32[128,256]{1,0:T(8,128)S(1)}, f32[2,128,128]{2,1,0:T(8,128)S(1)}) custom-call(s32[8,120]{1,0:T(8,128)S(1)} %bitcast.17, s32[8,120]{1,0:T(8,128)S(1)} %bitcast.18, s32[16,1]{1,0:T(8,128)S(1)} %pad.4.pat2_ref, f32[64,64,189]{2,1,0:T(8,128)S(1)} %bitcast.13, ...), custom_call_target="tpu_custom_call" | custom-call | tf_op jit(solution)/shard_map/weights/pallas_call | solution.py:216
  38.5 0.0 collective-permute-done.1
  38.5 1.9 %all-gather.2 = f32[4,64,128]{2,1,0:T(8,128)S(1)} all-gather(f32[2,64,128]{2,1,0:T(8,128)S(1)} %collective-permute-done.1), channel_id=4, replica_groups={{0,1},{2,3},{4,5},{6,7},{8,9},{10,11},{12,13},{14,15},{16,17},{18,19},{..., dimensions={0}, use_global_device_ids=true | all-gather | bytes 196608 | tf_op jit(solution)/shard_map/all_gather | solution.py:205
  40.4 0.0 collective-permute-done
  40.4 1.9 %all-gather.1 = f32[4,64,128]{2,1,0:T(8,128)S(1)} all-gather(f32[2,64,128]{2,1,0:T(8,128)S(1)} %collective-permute-done), channel_id=3, replica_groups={{0,1},{2,3},{4,5},{6,7},{8,9},{10,11},{12,13},{14,15},{16,17},{18,19},{..., dimensions={0}, use_global_device_ids=true | all-gather | bytes 196608 | tf_op jit(solution)/shard_map/all_gather | solution.py:205
  42.3 0.0 all-to-all-done
  42.3 2.0 %all-gather.3 = f32[16,32,128]{2,1,0:T(8,128)S(1)} all-gather(f32[8,32,128]{2,1,0:T(8,128)S(1)} %all-to-all-done), channel_id=5, replica_groups={{0,1},{2,3},{4,5},{6,7},{8,9},{10,11},{12,13},{14,15},{16,17},{18,19},{..., dimensions={0}, use_global_device_ids=true | all-gather | bytes 393216 | tf_op jit(solution)/shard_map/all_gather | solution.py:205
  44.3 0.0 copy-done.7
  44.3 0.0 copy-done.3
  44.3 3.9 %downward.1 = f32[8,64,512]{2,1,0:T(8,128)} custom-call(s32[1,1,1,8]{3,2,1,0:T(1,128)S(1)} %copy-done.7, s32[1]{0:T(128)} %bitcast.core_ref, bf16[8,128,256]{2,1,0:T(8,128)(2,1)S(1)} %get-tuple-element.13.high_ref, bf16[8,128,256]{2,1,0:T(8,128)(2,1)S(1)} %get-tuple-element.14.low_ref, f32[128,256]{1,0:T(8,128)S(1)} %get-tuple-element.15.own_ref, ...), custom_call_target="tpu_custom_call" | custom-call | tf_op jit(solution)/shard_map/downward/pallas_call | solution.py:238
  (2 shorter events, 0.0 us)
Async XLA Ops:
  0.0 44.3 %copy-start.7 = (s32[1,1,1,8]{3,2,1,0:T(1,128)S(1)}, s32[1,1,1,8]{3,2,1,0:T(1,128)}, u32[]{:S(2)}) copy-start(s32[1,1,1,8]{3,2,1,0:T(1,128)} %src2_ref.1) | copy-start | bytes 100
  0.8 1.2 %copy-start.1 = (f32[8,64,512]{2,1,0:T(8,128)S(1)}, f32[8,64,512]{2,1,0:T(8,128)}, u32[]{:S(2)}) copy-start(f32[8,64,512]{2,1,0:T(8,128)} %leaf_ref.1) | copy-start | bytes 3145732
  2.0 0.9 %copy-start.2 = (f32[8,64,64]{2,1,0:T(8,128)S(1)}, f32[8,64,64]{2,1,0:T(8,128)}, u32[]{:S(2)}) copy-start(f32[8,64,64]{2,1,0:T(8,128)} %m2m_ref.1) | copy-start | bytes 393220
  3.0 0.7 %copy-start.6 = (s32[1,1,4]{2,1,0:T(1,128)S(1)}, s32[1,1,4]{2,1,0:T(1,128)}, u32[]{:S(2)}) copy-start(s32[1,1,4]{2,1,0:T(1,128)} %counts_ref.1) | copy-start | bytes 52
  3.6 40.7 %copy-start.3 = (f32[8,64,64]{2,1,0:T(8,128)S(1)}, f32[8,64,64]{2,1,0:T(8,128)}, u32[]{:S(2)}) copy-start(f32[8,64,64]{2,1,0:T(8,128)} %l2l_ref.1) | copy-start | bytes 393220
  5.8 36.5 %all-to-all-start = ((f32[8,32,128]{2,1,0:T(8,128)}), f32[8,32,128]{2,1,0:T(8,128)S(1)}, u32[]{:S(2)}, u32[]{:S(2)}) async-start(f32[8,32,128]{2,1,0:T(8,128)} %get-tuple-element.18), calls=%async_computation | async-start | bytes 262144 | tf_op jit(solution)/shard_map/all_to_all | solution.py:212
  25.0 13.6 %collective-permute-start.1 = (f32[2,64,128]{2,1,0:T(8,128)S(1)}, f32[2,64,128]{2,1,0:T(8,128)S(1)}, u32[]{:S(2)}, u32[]{:S(2)}) collective-permute-start(f32[2,64,128]{2,1,0:T(8,128)S(1)} %get-tuple-element.19), channel_id=1, source_target_pairs={{16,0},{18,2},{20,4},{22,6},{24,8},{26,10},{28,12},{30,14},{32,16}... | collective-permute-start | bytes 196616 | tf_op jit(solution)/shard_map/ppermute | solution.py:202
  26.3 14.2 %collective-permute-start = (f32[2,64,128]{2,1,0:T(8,128)S(1)}, f32[2,64,128]{2,1,0:T(8,128)S(1)}, u32[]{:S(2)}, u32[]{:S(2)}) collective-permute-start(f32[2,64,128]{2,1,0:T(8,128)S(1)} %get-tuple-element.20), channel_id=1, source_target_pairs={{0,16},{1,33},{2,18},{3,35},{4,20},{5,37},{6,22},{7,39},{8,24},{9,... | collective-permute-start | bytes 196616 | tf_op jit(solution)/shard_map/ppermute | solution.py:202
  31.9 2.2 %copy-start = (f32[189,64,64]{0,2,1:T(8,128)S(1)}, f32[189,64,64]{0,2,1:T(8,128)}, u32[]{:S(2)}) copy-start(f32[189,64,64]{0,2,1:T(8,128)} %param.13) | copy-start | bytes 9289732
  34.1 0.7 %copy-start.4 = (s32[1,1,8,120]{3,2,1,0:T(8,128)S(1)}, s32[1,1,8,120]{3,2,1,0:T(8,128)}, u32[]{:S(2)}) copy-start(s32[1,1,8,120]{3,2,1,0:T(8,128)} %param.16) | copy-start | bytes 11524
  34.8 0.7 %copy-start.5 = (s32[1,1,8,120]{3,2,1,0:T(8,128)S(1)}, s32[1,1,8,120]{3,2,1,0:T(8,128)}, u32[]{:S(2)}) copy-start(s32[1,1,8,120]{3,2,1,0:T(8,128)} %param.17) | copy-start | bytes 11524

commit v2 on v1

v2 whole, which is shorter than its diff:
```python
import jax
import jax.numpy as jnp
from jax import lax
from jax.experimental import pallas as pl
from jax.experimental.pallas import tpu as pltpu
from jax.sharding import PartitionSpec as P

F32 = jnp.float32
BF16 = jnp.bfloat16
NT = (((1,), (1,)), ((), ()))


def split(x):
    high = x.astype(BF16)
    return high, (x - high.astype(F32)).astype(BF16)


def dot(a, b):
    return jnp.dot(a, b, preferred_element_type=F32)


def dot_nt(a, b):
    return lax.dot_general(a, b, NT, preferred_element_type=F32)


def dot3(a, b, product=dot):
    n = a[0].shape[0]
    both = product(jnp.concatenate(a, axis=0), b[0])
    return both[:n] + (product(a[0], b[1]) + both[n:])


def lanes(shape):
    return lax.broadcasted_iota(jnp.int32, shape, len(shape) - 1)


def rows(shape):
    return lax.broadcasted_iota(jnp.int32, shape, len(shape) - 2)


def four_blocks(low, high):
    none = jnp.zeros_like(low)
    left = jnp.concatenate([low, high, none, none], axis=0)
    right = jnp.concatenate([none, none, low, high], axis=0)
    return jnp.concatenate([left, right], axis=1)


def spread(pair):
    first = lanes(pair.shape) < 64
    turned = pltpu.roll(pair, 64, 1)
    result = []
    for side in (0, 1):
        low, high = (pair, turned) if side == 0 else (turned, pair)
        low = split(jnp.where(first, low, 0.0))
        high = split(jnp.where(first, 0.0, high))
        result.append((four_blocks(low[0], high[0]), four_blocks(low[1], high[1])))
    return result


def upward_kernel(
    blocks_hbm, counts_hbm, leaf_hbm, m2m_hbm, level1_ref, sends_ref, level2_ref,
    blocks, counts, leaf, m2m, ops, turned, grouped, twice, sems
):
    def copy(source, target, k):
        return pltpu.make_async_copy(source, target, sems.at[k])

    first_copies = [
        copy(m2m_hbm, m2m, 0),
        copy(leaf_hbm.at[0:4], leaf.at[0:4], 1),
        copy(leaf_hbm.at[4:8], leaf.at[4:8], 2),
        copy(blocks_hbm, blocks, 3),
        copy(counts_hbm, counts, 4),
    ]
    for c in first_copies:
        c.start()
    first_copies[0].wait()
    for o in range(8):
        ops[:, o * 64 : (o + 1) * 64] = m2m[o]
    operators = split(ops[...])
    level1 = jnp.zeros((64, 512), F32)
    for half in range(2):
        first_copies[1 + half].wait()
        operator = [part[:, 256 * half : 256 * half + 256] for part in operators]
        level1 = level1 + dot3(operator, split(leaf[4 * half : 4 * half + 4].reshape(256, 512)))
    level1_ref[...] = level1
    turned[...] = jnp.concatenate([level1, level1], axis=0).T
    for o in range(8):
        grouped[:, o * 64 : (o + 1) * 64] = turned[pl.ds(o, 64, stride=8), :][:, 0:64]
    level2 = dot3(operators, split(grouped[...]), dot_nt)
    first = lanes((32, 128)) < 64
    wide = jnp.concatenate([level2, level2], axis=1)
    packed = jnp.where(first, wide[0:32], wide[32:64])
    for member in range(16):
        level2_ref[member] = packed
    first = lanes((64, 128)) < 64
    for t in range(4):
        tile = level1[:, t * 128 : (t + 1) * 128]
        other = pltpu.roll(tile, 64, 1)
        twice[2 * t] = jnp.where(first, tile, other)
        twice[2 * t + 1] = jnp.where(first, other, tile)
    first_copies[3].wait()
    first_copies[4].wait()
    for w in range(4):
        count = counts[0, 0, w]
        left = jnp.where(count > 0, twice[blocks[0, 0, 0, w]], 0.0)
        right = jnp.where(count > 1, twice[blocks[0, 0, 1, w]], 0.0)
        sends_ref[w] = jnp.where(first, left, right)


def weights_kernel(
    src_ref, pat_ref, src2_ref, pat2_ref, m2l_hbm, level1_ref, high_ref, low_ref, own_ref, second_ref, table, second_s, m2l_ref, sems
):
    patterns = m2l_ref.shape[2]
    copies = [
        [
            pltpu.make_async_copy(m2l_hbm.at[part], m2l_ref.at[part], sems.at[4 * quarter + c])
            for c in range(4)
            for part in [pl.ds(16 * c + 4 * quarter, 4)]
        ]
        for quarter in range(4)
    ]
    for quarter in copies:
        for c in quarter:
            c.start()
    entries = src_ref.shape[1]
    code = src_ref[...] * 8 + rows((8, entries))
    pat = pat_ref[...]
    tally = jnp.zeros((128, patterns), F32)
    for r in range(8):
        sources = jnp.where(code[r : r + 1] == rows((128, entries)), 1.0, 0.0).astype(BF16)
        kinds = jnp.where(pat[r : r + 1] == rows((patterns, entries)), 1.0, 0.0).astype(BF16)
        tally = tally + dot_nt(sources, kinds)
    entries = src2_ref.shape[1]
    sources = jnp.where(src2_ref[...] == rows((16, entries)), 1.0, 0.0).astype(BF16)
    kinds = jnp.where(pat2_ref[...] == rows((patterns, entries)), 1.0, 0.0).astype(BF16)
    picks = jnp.concatenate([tally, dot_nt(sources, kinds)], axis=0).astype(BF16)
    for g in range(16):
        if g % 4 == 0:
            for c in copies[g // 4]:
                c.wait()
        high, low = split(jnp.concatenate([m2l_ref[16 * c + g] for c in range(4)], axis=0))
        operators = dot_nt(picks, high) + dot_nt(picks, low)
        table[g] = operators[0:128]
        for h in range(2):
            second_s[h, 16 * g : 16 * g + 16, :] = operators[128:144, 128 * h : 128 * h + 128]
    for s in range(8, 16):
        high, low = split(table[:, 8 * s : 8 * s + 8, :].reshape(128, 256))
        high_ref[s - 8] = high
        low_ref[s - 8] = low
    first = lanes((16, 128)) < 64
    for t in range(8):
        parts = []
        for h in range(2):
            a = second_s[h, pl.ds(2 * t, 16, stride=16), :]
            b = second_s[h, pl.ds(2 * t + 1, 16, stride=16), :]
            parts.append(jnp.where(first, a, pltpu.roll(b, 64, 1)))
            parts.append(jnp.where(first, pltpu.roll(a, 64, 1), b))
        second_ref[:, 128 * t : 128 * t + 128] = jnp.concatenate(split(jnp.concatenate(parts, axis=0)), axis=0)
    total = jnp.zeros((128, 256), F32)
    for t in range(4):
        both = spread(level1_ref[:, t * 128 : (t + 1) * 128])
        for side in (0, 1):
            s = 2 * t + side
            total = total + dot3(split(table[:, 8 * s : 8 * s + 8, :].reshape(128, 256)), both[side])
    own_ref[...] = total


def downward_kernel(
    high_ref, low_ref, own_ref, second_ref, came_ref, level2_ref, l2l_ref, out_ref, total_s
):
    total = own_ref[...]
    core = lax.axis_index("inner") % 2
    for w, (holder, place) in enumerate(((1, 0), (0, 0), (0, 2), (1, 2))):
        both = spread(came_ref[holder, place + core])
        for side in (0, 1):
            slot = 2 * w + side
            total = total + dot3((high_ref[slot], low_ref[slot]), both[side])
    for h in range(2):
        total_s[h] = total[:, 128 * h : 128 * h + 128]
    first = lanes((32, 128)) < 64
    sources = []
    for source in range(16):
        packed = level2_ref[source]
        turned = pltpu.roll(packed, 64, 1)
        sources += [jnp.where(first, packed, turned), jnp.where(first, turned, packed)]
    sources = split(jnp.concatenate(sources, axis=0))
    far = dot3((second_ref[0:64], second_ref[64:128]), sources)
    first = lanes((16, 128)) < 64
    local = []
    for t in range(4):
        parts = []
        for h in range(2):
            a = total_s[h, pl.ds(2 * t, 16, stride=8), :]
            b = total_s[h, pl.ds(2 * t + 1, 16, stride=8), :]
            parts.append(jnp.where(first, a, pltpu.roll(b, 64, 1)))
            parts.append(jnp.where(first, pltpu.roll(a, 64, 1), b))
        local.append(jnp.concatenate(parts, axis=0))
    local = jnp.concatenate(local, axis=1)
    operators = split(l2l_ref[...].reshape(512, 64))
    lowered = dot3(operators, split(far))
    first = lanes((64, 128)) < 64
    wide = [jnp.where(first, lowered[128 * t : 128 * t + 64], lowered[128 * t + 64 : 128 * t + 128]) for t in range(4)]
    place = 8 * (rows((512, 512)) % 64) + rows((512, 512)) // 64
    order = jnp.where(place == lanes((512, 512)), 1.0, 0.0).astype(BF16)
    head, tail = split(jnp.concatenate(wide, axis=1))
    local = local + (dot(head, order) + dot(tail, order))
    out_ref[...] = dot3(operators, split(local)).reshape(8, 64, 512)


SMEM = pl.BlockSpec(memory_space=pltpu.SMEM)
VMEM = pl.BlockSpec(memory_space=pltpu.VMEM)
HBM = pl.BlockSpec(memory_space=pltpu.HBM)
LIMIT = pltpu.CompilerParams(vmem_limit_bytes=24 * 1024 * 1024)


def in_hbm(x):
    return pltpu.with_memory_space_constraint(x, pltpu.HBM)


def upward(leaf_multipoles, m2m_ops, send_blocks, send_counts):
    return pl.pallas_call(
        upward_kernel,
        out_shape=[
            jax.ShapeDtypeStruct((64, 512), F32),
            jax.ShapeDtypeStruct((4, 64, 128), F32),
            jax.ShapeDtypeStruct((16, 32, 128), F32),
        ],
        in_specs=[HBM] * 4,
        out_specs=[VMEM] * 3,
        scratch_shapes=[
            pltpu.SMEM((1, 1, 2, 4), jnp.int32),
            pltpu.SMEM((1, 1, 4), jnp.int32),
            pltpu.VMEM((8, 64, 512), F32),
            pltpu.VMEM((8, 64, 64), F32),
            pltpu.VMEM((64, 512), F32),
            pltpu.VMEM((512, 128), F32),
            pltpu.VMEM((64, 512), F32),
            pltpu.VMEM((8, 64, 128), F32),
            pltpu.SemaphoreType.DMA((5,)),
        ],
        compiler_params=LIMIT,
        cost_estimate=pl.CostEstimate(flops=10**9, bytes_accessed=12 * 10**6, transcendentals=0),
        name="upward",
    )(
        in_hbm(jnp.transpose(send_blocks, (0, 1, 3, 2))),
        in_hbm(send_counts),
        in_hbm(leaf_multipoles),
        in_hbm(m2m_ops),
    )


def weights(list1_src, list1_pat, list2_src, list2_pat, m2l_ops, level1):
    patterns = m2l_ops.shape[0]
    return pl.pallas_call(
        weights_kernel,
        out_shape=[
            jax.ShapeDtypeStruct((8, 128, 256), BF16),
            jax.ShapeDtypeStruct((8, 128, 256), BF16),
            jax.ShapeDtypeStruct((128, 256), F32),
            jax.ShapeDtypeStruct((128, 1024), BF16),
        ],
        in_specs=[VMEM] * 4 + [HBM] + [VMEM],
        out_specs=[VMEM] * 4,
        scratch_shapes=[
            pltpu.VMEM((16, 128, 256), F32),
            pltpu.VMEM((2, 256, 128), F32),
            pltpu.VMEM((64, 64, patterns), F32),
            pltpu.SemaphoreType.DMA((16,)),
        ],
        compiler_params=LIMIT,
        name="weights",
    )(
        list1_src[0, 0],
        list1_pat[0, 0],
        list2_src[0, 0],
        list2_pat[0, 0],
        in_hbm(jnp.transpose(m2l_ops, (1, 2, 0))),
        level1,
    )


def downward(high, low, own, second, came, all_level2, l2l_ops):
    return pl.pallas_call(
        downward_kernel,
        out_shape=jax.ShapeDtypeStruct((8, 64, 512), F32),
        in_specs=[VMEM] * 7,
        out_specs=VMEM,
        scratch_shapes=[pltpu.VMEM((2, 128, 128), F32)],
        compiler_params=LIMIT,
        name="downward",
    )(high, low, own, second, came, all_level2, l2l_ops)


def on_device(
    leaf_multipoles, m2m_ops, l2l_ops, m2l_ops, send_blocks, send_counts, list1_src, list1_pat, list2_src, list2_pat
):
    doms, inners = lax.axis_size("dom"), lax.axis_size("inner")
    level1, sends, level2 = upward(leaf_multipoles, m2m_ops, send_blocks, send_counts)
    core = lax.axis_index("inner") % 2
    cores = [[2 * x, 2 * x + 1] for x in range(inners // 2)]

    def routed(block, side):
        route = []
        for d in range(doms):
            for i in range(inners):
                to = d + side * (1 + i % 2)
                if 0 <= to < doms:
                    route.append((d * inners + i, to * inners + i))
        return lax.ppermute(block, ("dom", "inner"), route)

    def both_cores(block):
        return lax.all_gather(block, "inner", axis=0, axis_index_groups=cores)

    all_level2 = lax.all_to_all(level2, "inner", 0, 0)
    chip_sends = both_cores(sends)
    upper = lax.dynamic_index_in_dim(chip_sends, 2 + core, 1, keepdims=False)
    lower = lax.dynamic_index_in_dim(chip_sends, 1 - core, 1, keepdims=False)
    came_up = routed(upper, 1)
    came_down = routed(lower, -1)
    operators = weights(list1_src, list1_pat, list2_src, list2_pat, m2l_ops, level1)
    came = both_cores(jnp.concatenate([came_up, came_down], axis=0))
    return downward(*operators, came, all_level2, l2l_ops)


def solution(mesh):
    placed = (
        P(None, None, ("dom", "inner")),
        P(),
        P(),
        P(),
        P("dom", "inner", None, None),
        P("dom", "inner", None),
        P("dom", "inner", None, None),
        P("dom", "inner", None, None),
        P("dom", "inner", None, None),
        P("dom", "inner", None, None),
    )
    return jax.shard_map(
        on_device,
        mesh=mesh,
        in_specs=placed,
        out_specs=P(None, None, ("dom", "inner")),
        check_vma=False,
    )
```

time: 48.6 us -> 35.6 us (0.73)
  blocking collectives: 17.6 us -> 4.52 us
  local copies, waits for them, and re-layouts: 7.92 us -> 0.03 us
  starting transfers between devices: 13.5 us -> 20.1 us
  Pallas kernels: 9.06 us -> 10.5 us
    all_gather x4 -> x2, blocking collectives: 17.6 us -> 4.52 us  [both_cores(): return lax.all_gather(block, 'inner', axis=0, axis_index_groups=cores)]
    all_to_all x1, starting transfers between devices: 7.31 us -> 17.5 us  [on_device(): all_level2 = lax.all_to_all(level2, 'inner', 0, 0)]
    unnamed x17 -> x10, local copies, waits for them, and re-layouts: 7.17 us -> 0.02 us
    ppermute x2, starting transfers between devices: 6.18 us -> 2.59 us  [routed(): return lax.ppermute(block, ('dom', 'inner'), route)]
    pallas_call x3, Pallas kernels: 9.06 us -> 10.5 us  [the longest x1 4.82 us: weights(): pl.pallas_call(weights_kernel, out_shape=[jax.ShapeDtypeStruct((8, 128, 2...]
    reshape x1 -> x0, local copies, waits for them, and re-layouts: 0.73 us -> none  [on_device(): list2_pat.reshape(8, 1)]
  transfers between devices with their start and end apart: 3 -> 3, of which waited for: 0 -> 0; matrix products, arithmetic and copies ran while one was open for 2% -> 0% of each run, Pallas kernels for 6% -> 14%
where the time goes in v2:
time: 35.6 us; the launch traced here: 35.3 us
  starting transfers between devices  20.1 us (56%)
  Pallas kernels  10.5 us (29%)
  blocking collectives  4.52 us (13%)
    all_to_all x1, starting transfers between devices, on_device(): all_level2 = lax.all_to_all(level2, 'inner', 0, 0)  17.5 us
    pallas_call x1, Pallas kernels, weights(): pl.pallas_call(weights_kernel, out_shape=[jax.ShapeDtypeStruct((8, 128, 2...  4.82 us
    all_gather x2, blocking collectives, both_cores(): return lax.all_gather(block, 'inner', axis=0, axis_index_groups=cores)  4.52 us
    pallas_call x1, Pallas kernels, upward(): pl.pallas_call(upward_kernel, out_shape=[jax.ShapeDtypeStruct((64, 512),...  2.9 us
    pallas_call x1, Pallas kernels, downward(): pl.pallas_call(downward_kernel, out_shape=jax.ShapeDtypeStruct((8, 64, 51...  2.8 us
    ppermute x2, starting transfers between devices, routed(): return lax.ppermute(block, ('dom', 'inner'), route)  2.59 us
  transfers between devices with their start and end apart: 3, of which 0 were waited for; matrix products, arithmetic and copies ran while one was open for 0% of the time, Pallas kernels for 14%

profile of v2, /device:TPU:1, one launch (start us, length us, event | category | flops | bytes accessed | tf_op | source)
XLA Modules:
  0.0 35.3 jit_solution(13432983543136744801)
XLA Ops:
  0.0 0.0 copy-start.4
  0.0 0.0 copy-start.3
  0.0 0.0 copy-start.2
  0.0 0.0 copy-start.1
  0.0 0.0 copy-start
  0.0 2.9 %upward.1 = (f32[64,512]{1,0:T(8,128)S(1)}, f32[4,64,128]{2,1,0:T(8,128)S(1)}, f32[16,32,128]{2,1,0:T(8,128)}) custom-call(s32[1,1,2,4]{3,2,1,0:T(2,128)} %bitcast.19, s32[1,1,4]{2,1,0:T(1,128)} %counts_hbm.1, f32[8,64,512]{2,1,0:T(8,128)} %leaf_hbm.1, f32[8,64,64]{2,1,0:T(8,128)} %m2m_hbm.1), custom_call_target="tpu_custom_call" | custom-call | flops 1000000000 | bytes 12000000 | tf_op jit(solution)/shard_map/upward/pallas_call | solution.py:220
  2.9 17.5 %all-to-all-start = ((f32[16,32,128]{2,1,0:T(8,128)}), f32[16,32,128]{2,1,0:T(8,128)S(1)}, u32[]{:S(2)}, u32[]{:S(2)}) async-start(f32[16,32,128]{2,1,0:T(8,128)} %get-tuple-element.18), calls=%async_computation | async-start | bytes 524288 | tf_op jit(solution)/shard_map/all_to_all | solution.py:313
  20.4 2.0 %all-gather = f32[8,64,128]{2,1,0:T(8,128)S(1)} all-gather(f32[4,64,128]{2,1,0:T(8,128)S(1)} %get-tuple-element.17), channel_id=2, replica_groups={{0,1},{2,3},{4,5},{6,7},{8,9},{10,11},{12,13},{14,15},{16,17},{18,19},{..., dimensions={0}, use_global_device_ids=true | all-gather | bytes 393216 | tf_op jit(solution)/shard_map/all_gather | solution.py:311
  22.4 1.3 %collective-permute-start = (f32[2,64,128]{2,1,0:T(8,128)S(1)}, f32[2,64,128]{2,1,0:T(8,128)S(1)}, u32[]{:S(2)}, u32[]{:S(2)}) collective-permute-start(f32[2,64,128]{2,1,0:T(8,128)S(1)} %get-tuple-element.19), channel_id=1, source_target_pairs={{0,16},{1,33},{2,18},{3,35},{4,20},{5,37},{6,22},{7,39},{8,24},{9,... | collective-permute-start | bytes 196616 | tf_op jit(solution)/shard_map/ppermute | solution.py:308
  23.7 1.3 %collective-permute-start.1 = (f32[2,64,128]{2,1,0:T(8,128)S(1)}, f32[2,64,128]{2,1,0:T(8,128)S(1)}, u32[]{:S(2)}, u32[]{:S(2)}) collective-permute-start(f32[2,64,128]{2,1,0:T(8,128)S(1)} %get-tuple-element.20), channel_id=1, source_target_pairs={{16,0},{18,2},{20,4},{22,6},{24,8},{26,10},{28,12},{30,14},{32,16}... | collective-permute-start | bytes 196616 | tf_op jit(solution)/shard_map/ppermute | solution.py:308
  25.0 0.0 copy-done.4
  25.0 0.0 copy-done.3
  25.0 0.0 copy-done.2
  25.0 0.0 copy-done.1
  25.1 4.8 %weights.1 = (bf16[8,128,256]{2,1,0:T(8,128)(2,1)S(1)}, bf16[8,128,256]{2,1,0:T(8,128)(2,1)S(1)}, f32[128,256]{1,0:T(8,128)S(1)}, bf16[128,1024]{1,0:T(8,128)(2,1)S(1)}) custom-call(s32[8,120]{1,0:T(8,128)S(1)} %bitcast.13, s32[8,120]{1,0:T(8,128)S(1)} %bitcast.14, s32[1,8]{1,0:T(1,128)S(1)} %bitcast.15, s32[1,8]{1,0:T(1,128)S(1)} %bitcast.16, ...), custom_call_target="tpu_custom_call" | custom-call | tf_op jit(solution)/shard_map/weights/pallas_call | solution.py:253
  29.9 0.0 collective-permute-done
  29.9 0.0 collective-permute-done.1
  29.9 2.5 %all-gather.1 = f32[8,64,128]{2,1,0:T(8,128)S(1)} all-gather(f32[4,64,128]{2,1,0:T(8,128)S(1)} %pad_maximum_fusion), channel_id=3, replica_groups={{0,1},{2,3},{4,5},{6,7},{8,9},{10,11},{12,13},{14,15},{16,17},{18,19},{..., dimensions={0}, use_global_device_ids=true | all-gather | bytes 393216 | tf_op jit(solution)/shard_map/all_gather | solution.py:311
  32.5 0.0 all-to-all-done.level2_ref
  32.5 0.0 copy-done
  32.5 2.8 %downward.1 = f32[8,64,512]{2,1,0:T(8,128)} custom-call(bf16[8,128,256]{2,1,0:T(8,128)(2,1)S(1)} %get-tuple-element.13.high_ref, bf16[8,128,256]{2,1,0:T(8,128)(2,1)S(1)} %get-tuple-element.14.low_ref, f32[128,256]{1,0:T(8,128)S(1)} %get-tuple-element.15.own_ref, bf16[128,1024]{1,0:T(8,128)(2,1)S(1)} %get-tuple-element.16.second_ref, ...), custom_call_target="tpu_custom_call" | custom-call | tf_op jit(solution)/shard_map/downward/pallas_call | solution.py:282
  (2 shorter events, 0.0 us)
Async XLA Ops:
  0.0 25.0 %copy-start.4 = (s32[1,1,1,8]{3,2,1,0:T(1,128)S(1)}, s32[1,1,1,8]{3,2,1,0:T(1,128)}, u32[]{:S(2)}) copy-start(s32[1,1,1,8]{3,2,1,0:T(1,128)} %param.19) | copy-start | bytes 100
  0.0 25.0 %copy-start.3 = (s32[1,1,1,8]{3,2,1,0:T(1,128)S(1)}, s32[1,1,1,8]{3,2,1,0:T(1,128)}, u32[]{:S(2)}) copy-start(s32[1,1,1,8]{3,2,1,0:T(1,128)} %param.18) | copy-start | bytes 100
  0.0 25.0 %copy-start.2 = (s32[1,1,8,120]{3,2,1,0:T(8,128)S(1)}, s32[1,1,8,120]{3,2,1,0:T(8,128)}, u32[]{:S(2)}) copy-start(s32[1,1,8,120]{3,2,1,0:T(8,128)} %param.17) | copy-start | bytes 11524
  0.0 25.0 %copy-start.1 = (s32[1,1,8,120]{3,2,1,0:T(8,128)S(1)}, s32[1,1,8,120]{3,2,1,0:T(8,128)}, u32[]{:S(2)}) copy-start(s32[1,1,8,120]{3,2,1,0:T(8,128)} %param.16) | copy-start | bytes 11524
  0.0 32.5 %copy-start = (f32[8,64,64]{2,1,0:T(8,128)S(1)}, f32[8,64,64]{2,1,0:T(8,128)}, u32[]{:S(2)}) copy-start(f32[8,64,64]{2,1,0:T(8,128)} %l2l_ref.1) | copy-start | bytes 393220
  2.9 29.5 %all-to-all-start = ((f32[16,32,128]{2,1,0:T(8,128)}), f32[16,32,128]{2,1,0:T(8,128)S(1)}, u32[]{:S(2)}, u32[]{:S(2)}) async-start(f32[16,32,128]{2,1,0:T(8,128)} %get-tuple-element.18), calls=%async_computation | async-start | bytes 524288 | tf_op jit(solution)/shard_map/all_to_all | solution.py:313
  22.4 7.5 %collective-permute-start = (f32[2,64,128]{2,1,0:T(8,128)S(1)}, f32[2,64,128]{2,1,0:T(8,128)S(1)}, u32[]{:S(2)}, u32[]{:S(2)}) collective-permute-start(f32[2,64,128]{2,1,0:T(8,128)S(1)} %get-tuple-element.19), channel_id=1, source_target_pairs={{0,16},{1,33},{2,18},{3,35},{4,20},{5,37},{6,22},{7,39},{8,24},{9,... | collective-permute-start | bytes 196616 | tf_op jit(solution)/shard_map/ppermute | solution.py:308
  23.7 6.2 %collective-permute-start.1 = (f32[2,64,128]{2,1,0:T(8,128)S(1)}, f32[2,64,128]{2,1,0:T(8,128)S(1)}, u32[]{:S(2)}, u32[]{:S(2)}) collective-permute-start(f32[2,64,128]{2,1,0:T(8,128)S(1)} %get-tuple-element.20), channel_id=1, source_target_pairs={{16,0},{18,2},{20,4},{22,6},{24,8},{26,10},{28,12},{30,14},{32,16}... | collective-permute-start | bytes 196616 | tf_op jit(solution)/shard_map/ppermute | solution.py:308

commit v3 on v2

--- a/solution.py
+++ b/solution.py
@@ -27,6 +27,16 @@
     n = a[0].shape[0]
     both = product(jnp.concatenate(a, axis=0), b[0])
     return both[:n] + (product(a[0], b[1]) + both[n:])
+
+
+def dot3_sum(pairs):
+    left = [x for a, _ in pairs for x in (a[0], a[0], a[1])]
+    right = [x for _, b in pairs for x in (b[0], b[1], b[0])]
+    return dot(jnp.concatenate(left, axis=1), jnp.concatenate(right, axis=0))
+
+
+def dot3k(a, b):
+    return dot3_sum([(a, b)])
 
 
 def lanes(shape):
@@ -89,7 +99,7 @@
     first = lanes((32, 128)) < 64
     wide = jnp.concatenate([level2, level2], axis=1)
     packed = jnp.where(first, wide[0:32], wide[32:64])
-    for member in range(16):
+    for member in range(8):
         level2_ref[member] = packed
     first = lanes((64, 128)) < 64
     for t in range(4):
@@ -165,25 +175,28 @@
 
 
 def downward_kernel(
-    high_ref, low_ref, own_ref, second_ref, came_ref, level2_ref, l2l_ref, out_ref, total_s
+    high_ref, low_ref, own_ref, second_ref, came_ref, l2l_ref, out_ref, total_s
 ):
-    total = own_ref[...]
+    pairs = []
     core = lax.axis_index("inner") % 2
     for w, (holder, place) in enumerate(((1, 0), (0, 0), (0, 2), (1, 2))):
         both = spread(came_ref[holder, place + core])
         for side in (0, 1):
             slot = 2 * w + side
-            total = total + dot3((high_ref[slot], low_ref[slot]), both[side])
+            pairs.append(((high_ref[slot], low_ref[slot]), both[side]))
+
+    total = own_ref[...] + dot3_sum(pairs)
     for h in range(2):
         total_s[h] = total[:, 128 * h : 128 * h + 128]
     first = lanes((32, 128)) < 64
     sources = []
     for source in range(16):
-        packed = level2_ref[source]
+        chip = source // 2
+        packed = came_ref[source % 2, 4 + chip // 2, 32 * (chip % 2) : 32 * (chip % 2) + 32, :]
         turned = pltpu.roll(packed, 64, 1)
         sources += [jnp.where(first, packed, turned), jnp.where(first, turned, packed)]
     sources = split(jnp.concatenate(sources, axis=0))
-    far = dot3((second_ref[0:64], second_ref[64:128]), sources)
+    far = dot3k((second_ref[0:64], second_ref[64:128]), sources)
     first = lanes((16, 128)) < 64
     local = []
     for t in range(4):
@@ -196,14 +209,14 @@
         local.append(jnp.concatenate(parts, axis=0))
     local = jnp.concatenate(local, axis=1)
     operators = split(l2l_ref[...].reshape(512, 64))
-    lowered = dot3(operators, split(far))
+    lowered = dot3k(operators, split(far))
     first = lanes((64, 128)) < 64
     wide = [jnp.where(first, lowered[128 * t : 128 * t + 64], lowered[128 * t + 64 : 128 * t + 128]) for t in range(4)]
     place = 8 * (rows((512, 512)) % 64) + rows((512, 512)) // 64
     order = jnp.where(place == lanes((512, 512)), 1.0, 0.0).astype(BF16)
     head, tail = split(jnp.concatenate(wide, axis=1))
-    local = local + (dot(head, order) + dot(tail, order))
-    out_ref[...] = dot3(operators, split(local)).reshape(8, 64, 512)
+    local = local + dot(jnp.concatenate([head, tail], axis=1), jnp.concatenate([order, order], axis=0))
+    out_ref[...] = dot3k(operators, split(local)).reshape(8, 64, 512)
 
 
 SMEM = pl.BlockSpec(memory_space=pltpu.SMEM)
@@ -222,7 +235,7 @@
         out_shape=[
             jax.ShapeDtypeStruct((64, 512), F32),
             jax.ShapeDtypeStruct((4, 64, 128), F32),
-            jax.ShapeDtypeStruct((16, 32, 128), F32),
+            jax.ShapeDtypeStruct((8, 32, 128), F32),
         ],
         in_specs=[HBM] * 4,
         out_specs=[VMEM] * 3,
@@ -278,16 +291,16 @@
     )
 
 
-def downward(high, low, own, second, came, all_level2, l2l_ops):
+def downward(high, low, own, second, came, l2l_ops):
     return pl.pallas_call(
         downward_kernel,
         out_shape=jax.ShapeDtypeStruct((8, 64, 512), F32),
-        in_specs=[VMEM] * 7,
+        in_specs=[VMEM] * 6,
         out_specs=VMEM,
         scratch_shapes=[pltpu.VMEM((2, 128, 128), F32)],
         compiler_params=LIMIT,
         name="downward",
-    )(high, low, own, second, came, all_level2, l2l_ops)
+    )(high, low, own, second, came, l2l_ops)
 
 
 def on_device(
@@ -310,15 +323,16 @@
     def both_cores(block):
         return lax.all_gather(block, "inner", axis=0, axis_index_groups=cores)
 
-    all_level2 = lax.all_to_all(level2, "inner", 0, 0)
+    chips = [[2 * x + c for x in range(inners // 2)] for c in range(2)]
+    own_side = lax.all_to_all(level2, "inner", 0, 0, axis_index_groups=chips)
     chip_sends = both_cores(sends)
     upper = lax.dynamic_index_in_dim(chip_sends, 2 + core, 1, keepdims=False)
     lower = lax.dynamic_index_in_dim(chip_sends, 1 - core, 1, keepdims=False)
     came_up = routed(upper, 1)
     came_down = routed(lower, -1)
     operators = weights(list1_src, list1_pat, list2_src, list2_pat, m2l_ops, level1)
-    came = both_cores(jnp.concatenate([came_up, came_down], axis=0))
-    return downward(*operators, came, all_level2, l2l_ops)
+    came = jnp.concatenate([came_up, came_down, own_side.reshape(4, 64, 128)], axis=0)
+    return downward(*operators, both_cores(came), l2l_ops)
 
 
 def solution(mesh):

time: 35.6 us -> 35.4 us (level)
  blocking collectives: 4.52 us -> 14.7 us
  starting transfers between devices: 20.1 us -> 10 us
    all_gather x2, blocking collectives: 4.52 us -> 14.7 us  [both_cores(): return lax.all_gather(block, 'inner', axis=0, axis_index_groups=cores)]
    all_to_all x1, starting transfers between devices: 17.5 us -> 7.45 us  [on_device(): own_side = lax.all_to_all(level2, 'inner', 0, 0, axis_index_groups=chips)]
where the time goes in v3:
time: 35.4 us; the launch traced here: 35.1 us
  blocking collectives  14.7 us (42%)
  Pallas kernels  10.2 us (29%)
  starting transfers between devices  10 us (28%)
    all_gather x2, blocking collectives, both_cores(): return lax.all_gather(block, 'inner', axis=0, axis_index_groups=cores)  14.7 us
    all_to_all x1, starting transfers between devices, on_device(): own_side = lax.all_to_all(level2, 'inner', 0, 0, axis_index_groups=chips)  7.45 us
    pallas_call x1, Pallas kernels, weights(): pl.pallas_call(weights_kernel, out_shape=[jax.ShapeDtypeStruct((8, 128, 2...  4.82 us
    pallas_call x1, Pallas kernels, upward(): pl.pallas_call(upward_kernel, out_shape=[jax.ShapeDtypeStruct((64, 512),...  2.83 us
    ppermute x2, starting transfers between devices, routed(): return lax.ppermute(block, ('dom', 'inner'), route)  2.59 us
    pallas_call x1, Pallas kernels, downward(): pl.pallas_call(downward_kernel, out_shape=jax.ShapeDtypeStruct((8, 64, 51...  2.57 us
  transfers between devices with their start and end apart: 3, of which 0 were waited for; matrix products, arithmetic and copies ran while one was open for 0% of the time, Pallas kernels for 14%

profile of v3, /device:TPU:1, one launch (start us, length us, event | category | flops | bytes accessed | tf_op | source)
XLA Modules:
  0.0 35.1 jit_solution(597731458405995569)
XLA Ops:
  0.0 0.0 copy-start.4
  0.0 0.0 copy-start.3
  0.0 0.0 copy-start.2
  0.0 0.0 copy-start.1
  0.0 2.8 %upward.1 = (f32[64,512]{1,0:T(8,128)S(1)}, f32[4,64,128]{2,1,0:T(8,128)S(1)}, f32[8,32,128]{2,1,0:T(8,128)}) custom-call(s32[1,1,2,4]{3,2,1,0:T(2,128)} %bitcast.21, s32[1,1,4]{2,1,0:T(1,128)} %counts_hbm.1, f32[8,64,512]{2,1,0:T(8,128)} %leaf_hbm.1, f32[8,64,64]{2,1,0:T(8,128)} %m2m_hbm.1), custom_call_target="tpu_custom_call" | custom-call | flops 1000000000 | bytes 12000000 | tf_op jit(solution)/shard_map/upward/pallas_call | solution.py:233
  2.9 0.0 copy-start
  2.9 7.5 %all-to-all-start = ((f32[8,32,128]{2,1,0:T(8,128)}), f32[8,32,128]{2,1,0:T(8,128)S(1)}, u32[]{:S(2)}, u32[]{:S(2)}) async-start(f32[8,32,128]{2,1,0:T(8,128)} %get-tuple-element.18), calls=%async_computation | async-start | bytes 262144 | tf_op jit(solution)/shard_map/all_to_all | solution.py:327
  10.3 11.9 %all-gather = f32[8,64,128]{2,1,0:T(8,128)S(1)} all-gather(f32[4,64,128]{2,1,0:T(8,128)S(1)} %get-tuple-element.17), channel_id=2, replica_groups={{0,1},{2,3},{4,5},{6,7},{8,9},{10,11},{12,13},{14,15},{16,17},{18,19},{..., dimensions={0}, use_global_device_ids=true | all-gather | bytes 393216 | tf_op jit(solution)/shard_map/all_gather | solution.py:324
  22.2 1.3 %collective-permute-start = (f32[2,64,128]{2,1,0:T(8,128)S(1)}, f32[2,64,128]{2,1,0:T(8,128)S(1)}, u32[]{:S(2)}, u32[]{:S(2)}) collective-permute-start(f32[2,64,128]{2,1,0:T(8,128)S(1)} %get-tuple-element.19), channel_id=1, source_target_pairs={{0,16},{1,33},{2,18},{3,35},{4,20},{5,37},{6,22},{7,39},{8,24},{9,... | collective-permute-start | bytes 196616 | tf_op jit(solution)/shard_map/ppermute | solution.py:321
  23.5 1.3 %collective-permute-start.1 = (f32[2,64,128]{2,1,0:T(8,128)S(1)}, f32[2,64,128]{2,1,0:T(8,128)S(1)}, u32[]{:S(2)}, u32[]{:S(2)}) collective-permute-start(f32[2,64,128]{2,1,0:T(8,128)S(1)} %get-tuple-element.20), channel_id=1, source_target_pairs={{16,0},{18,2},{20,4},{22,6},{24,8},{26,10},{28,12},{30,14},{32,16}... | collective-permute-start | bytes 196616 | tf_op jit(solution)/shard_map/ppermute | solution.py:321
  24.8 0.0 copy-done.4
  24.8 0.0 copy-done.3
  24.8 0.0 copy-done.2
  24.8 0.0 copy-done.1
  24.8 4.8 %weights.1 = (bf16[8,128,256]{2,1,0:T(8,128)(2,1)S(1)}, bf16[8,128,256]{2,1,0:T(8,128)(2,1)S(1)}, f32[128,256]{1,0:T(8,128)S(1)}, bf16[128,1024]{1,0:T(8,128)(2,1)S(1)}) custom-call(s32[8,120]{1,0:T(8,128)S(1)} %bitcast.14, s32[8,120]{1,0:T(8,128)S(1)} %bitcast.15, s32[1,8]{1,0:T(1,128)S(1)} %bitcast.16, s32[1,8]{1,0:T(1,128)S(1)} %bitcast.17, ...), custom_call_target="tpu_custom_call" | custom-call | tf_op jit(solution)/shard_map/weights/pallas_call | solution.py:266
  29.7 0.0 collective-permute-done
  29.7 0.0 collective-permute-done.1
  29.7 0.0 all-to-all-done
  29.7 2.8 %all-gather.1 = f32[16,64,128]{2,1,0:T(8,128)S(1)} all-gather(f32[8,64,128]{2,1,0:T(8,128)S(1)} %pad_maximum_fusion), channel_id=3, replica_groups={{0,1},{2,3},{4,5},{6,7},{8,9},{10,11},{12,13},{14,15},{16,17},{18,19},{..., dimensions={0}, use_global_device_ids=true | all-gather | bytes 786432 | tf_op jit(solution)/shard_map/all_gather | solution.py:324
  32.6 0.0 copy-done
  32.6 2.6 %downward.1 = f32[8,64,512]{2,1,0:T(8,128)} custom-call(bf16[8,128,256]{2,1,0:T(8,128)(2,1)S(1)} %get-tuple-element.13.high_ref, bf16[8,128,256]{2,1,0:T(8,128)(2,1)S(1)} %get-tuple-element.14.low_ref, f32[128,256]{1,0:T(8,128)S(1)} %get-tuple-element.15.own_ref, bf16[128,1024]{1,0:T(8,128)(2,1)S(1)} %get-tuple-element.16.second_ref, ...), custom_call_target="tpu_custom_call" | custom-call | tf_op jit(solution)/shard_map/downward/pallas_call | solution.py:295
  (2 shorter events, 0.0 us)
Async XLA Ops:
  0.0 24.8 %copy-start.4 = (s32[1,1,1,8]{3,2,1,0:T(1,128)S(1)}, s32[1,1,1,8]{3,2,1,0:T(1,128)}, u32[]{:S(2)}) copy-start(s32[1,1,1,8]{3,2,1,0:T(1,128)} %param.19) | copy-start | bytes 100
  0.0 24.8 %copy-start.3 = (s32[1,1,1,8]{3,2,1,0:T(1,128)S(1)}, s32[1,1,1,8]{3,2,1,0:T(1,128)}, u32[]{:S(2)}) copy-start(s32[1,1,1,8]{3,2,1,0:T(1,128)} %param.18) | copy-start | bytes 100
  0.0 24.8 %copy-start.2 = (s32[1,1,8,120]{3,2,1,0:T(8,128)S(1)}, s32[1,1,8,120]{3,2,1,0:T(8,128)}, u32[]{:S(2)}) copy-start(s32[1,1,8,120]{3,2,1,0:T(8,128)} %param.17) | copy-start | bytes 11524
  0.0 24.8 %copy-start.1 = (s32[1,1,8,120]{3,2,1,0:T(8,128)S(1)}, s32[1,1,8,120]{3,2,1,0:T(8,128)}, u32[]{:S(2)}) copy-start(s32[1,1,8,120]{3,2,1,0:T(8,128)} %param.16) | copy-start | bytes 11524
  2.9 29.7 %copy-start = (f32[8,64,64]{2,1,0:T(8,128)S(1)}, f32[8,64,64]{2,1,0:T(8,128)}, u32[]{:S(2)}) copy-start(f32[8,64,64]{2,1,0:T(8,128)} %l2l_ref.1) | copy-start | bytes 393220
  2.9 26.8 %all-to-all-start = ((f32[8,32,128]{2,1,0:T(8,128)}), f32[8,32,128]{2,1,0:T(8,128)S(1)}, u32[]{:S(2)}, u32[]{:S(2)}) async-start(f32[8,32,128]{2,1,0:T(8,128)} %get-tuple-element.18), calls=%async_computation | async-start | bytes 262144 | tf_op jit(solution)/shard_map/all_to_all | solution.py:327
  22.2 7.5 %collective-permute-start = (f32[2,64,128]{2,1,0:T(8,128)S(1)}, f32[2,64,128]{2,1,0:T(8,128)S(1)}, u32[]{:S(2)}, u32[]{:S(2)}) collective-permute-start(f32[2,64,128]{2,1,0:T(8,128)S(1)} %get-tuple-element.19), channel_id=1, source_target_pairs={{0,16},{1,33},{2,18},{3,35},{4,20},{5,37},{6,22},{7,39},{8,24},{9,... | collective-permute-start | bytes 196616 | tf_op jit(solution)/shard_map/ppermute | solution.py:321
  23.5 6.2 %collective-permute-start.1 = (f32[2,64,128]{2,1,0:T(8,128)S(1)}, f32[2,64,128]{2,1,0:T(8,128)S(1)}, u32[]{:S(2)}, u32[]{:S(2)}) collective-permute-start(f32[2,64,128]{2,1,0:T(8,128)S(1)} %get-tuple-element.20), channel_id=1, source_target_pairs={{16,0},{18,2},{20,4},{22,6},{24,8},{26,10},{28,12},{30,14},{32,16}... | collective-permute-start | bytes 196616 | tf_op jit(solution)/shard_map/ppermute | solution.py:321

commit v4 on v3

--- a/solution.py
+++ b/solution.py
@@ -66,9 +66,22 @@
     return result
 
 
+EARLY = 8
+
+
+def translate(picks, m2l_ref, table_ref, second_ref):
+    for g in range(m2l_ref.shape[0] // 4):
+        high, low = split(m2l_ref[4 * g : 4 * g + 4].reshape(256, m2l_ref.shape[2]))
+        operators = dot_nt(jnp.concatenate([picks, picks], axis=1), jnp.concatenate([high, low], axis=1))
+        table_ref[g] = operators[0:128]
+        for h in range(2):
+            second_ref[h, 16 * g : 16 * g + 16, :] = operators[128:144, 128 * h : 128 * h + 128]
+
+
 def upward_kernel(
-    blocks_hbm, counts_hbm, leaf_hbm, m2m_hbm, level1_ref, sends_ref, level2_ref,
-    blocks, counts, leaf, m2m, ops, turned, grouped, twice, sems
+    blocks_hbm, counts_hbm, leaf_hbm, m2m_hbm, src_hbm, pat_hbm, src2_hbm, pat2_hbm, m2l_hbm,
+    level1_ref, sends_ref, level2_hbm, picks_ref, table_ref, second_ref,
+    blocks, counts, leaf, m2m, src_ref, pat_ref, src2_ref, pat2_ref, m2l_ref, ops, turned, grouped, twice, copies, sems
 ):
     def copy(source, target, k):
         return pltpu.make_async_copy(source, target, sems.at[k])
@@ -80,7 +93,11 @@
         copy(blocks_hbm, blocks, 3),
         copy(counts_hbm, counts, 4),
     ]
-    for c in first_copies:
+    list_copies = [
+        copy(src_hbm, src_ref, 5), copy(pat_hbm, pat_ref, 6), copy(src2_hbm, src2_ref, 7), copy(pat2_hbm, pat2_ref, 8)
+    ]
+    m2l_copy = copy(m2l_hbm.at[0 : 4 * EARLY], m2l_ref, 10)
+    for c in first_copies + list_copies + [m2l_copy]:
         c.start()
     first_copies[0].wait()
     for o in range(8):
@@ -100,7 +117,9 @@
     wide = jnp.concatenate([level2, level2], axis=1)
     packed = jnp.where(first, wide[0:32], wide[32:64])
     for member in range(8):
-        level2_ref[member] = packed
+        copies[member] = packed
+    level2_copy = copy(copies, level2_hbm, 9)
+    level2_copy.start()
     first = lanes((64, 128)) < 64
     for t in range(4):
         tile = level1[:, t * 128 : (t + 1) * 128]
@@ -114,23 +133,9 @@
         left = jnp.where(count > 0, twice[blocks[0, 0, 0, w]], 0.0)
         right = jnp.where(count > 1, twice[blocks[0, 0, 1, w]], 0.0)
         sends_ref[w] = jnp.where(first, left, right)
-
-
-def weights_kernel(
-    src_ref, pat_ref, src2_ref, pat2_ref, m2l_hbm, level1_ref, high_ref, low_ref, own_ref, second_ref, table, second_s, m2l_ref, sems
-):
+    for c in list_copies:
+        c.wait()
     patterns = m2l_ref.shape[2]
-    copies = [
-        [
-            pltpu.make_async_copy(m2l_hbm.at[part], m2l_ref.at[part], sems.at[4 * quarter + c])
-            for c in range(4)
-            for part in [pl.ds(16 * c + 4 * quarter, 4)]
-        ]
-        for quarter in range(4)
-    ]
-    for quarter in copies:
-        for c in quarter:
-            c.start()
     entries = src_ref.shape[1]
     code = src_ref[...] * 8 + rows((8, entries))
     pat = pat_ref[...]
@@ -143,25 +148,35 @@
     sources = jnp.where(src2_ref[...] == rows((16, entries)), 1.0, 0.0).astype(BF16)
     kinds = jnp.where(pat2_ref[...] == rows((patterns, entries)), 1.0, 0.0).astype(BF16)
     picks = jnp.concatenate([tally, dot_nt(sources, kinds)], axis=0).astype(BF16)
-    for g in range(16):
-        if g % 4 == 0:
-            for c in copies[g // 4]:
-                c.wait()
-        high, low = split(jnp.concatenate([m2l_ref[16 * c + g] for c in range(4)], axis=0))
-        operators = dot_nt(picks, high) + dot_nt(picks, low)
-        table[g] = operators[0:128]
-        for h in range(2):
-            second_s[h, 16 * g : 16 * g + 16, :] = operators[128:144, 128 * h : 128 * h + 128]
+    picks_ref[...] = picks
+    m2l_copy.wait()
+    translate(picks, m2l_ref, table_ref, second_ref)
+    level2_copy.wait()
+
+
+def weights_kernel(
+    picks_ref, table_ref, early_ref, m2l_hbm, level1_ref, high_ref, low_ref, own_ref, second_ref,
+    table, second_s, m2l_ref, sem
+):
+    m2l_copy = pltpu.make_async_copy(m2l_hbm.at[4 * EARLY : 64], m2l_ref, sem)
+    m2l_copy.start()
+    m2l_copy.wait()
+    translate(picks_ref[...], m2l_ref, table, second_s)
+
+    def operators(s):
+        place = pl.ds(8 * s, 8)
+        return split(jnp.concatenate([table_ref[:, place, :], table[:, place, :]], axis=0).reshape(128, 256))
+
     for s in range(8, 16):
-        high, low = split(table[:, 8 * s : 8 * s + 8, :].reshape(128, 256))
-        high_ref[s - 8] = high
-        low_ref[s - 8] = low
+        high_ref[s - 8], low_ref[s - 8] = operators(s)
     first = lanes((16, 128)) < 64
     for t in range(8):
         parts = []
         for h in range(2):
-            a = second_s[h, pl.ds(2 * t, 16, stride=16), :]
-            b = second_s[h, pl.ds(2 * t + 1, 16, stride=16), :]
+            a, b = (
+                jnp.concatenate([ref[h, pl.ds(s, ref.shape[1] // 16, stride=16), :] for ref in (early_ref, second_s)], axis=0)
+                for s in (2 * t, 2 * t + 1)
+            )
             parts.append(jnp.where(first, a, pltpu.roll(b, 64, 1)))
             parts.append(jnp.where(first, pltpu.roll(a, 64, 1), b))
         second_ref[:, 128 * t : 128 * t + 128] = jnp.concatenate(split(jnp.concatenate(parts, axis=0)), axis=0)
@@ -169,17 +184,16 @@
     for t in range(4):
         both = spread(level1_ref[:, t * 128 : (t + 1) * 128])
         for side in (0, 1):
-            s = 2 * t + side
-            total = total + dot3(split(table[:, 8 * s : 8 * s + 8, :].reshape(128, 256)), both[side])
+            total = total + dot3(operators(2 * t + side), both[side])
     own_ref[...] = total
 
 
 def downward_kernel(
-    high_ref, low_ref, own_ref, second_ref, came_ref, l2l_ref, out_ref, total_s
+    high_ref, low_ref, own_ref, second_ref, came_ref, l2l_ref, out_ref, total_s, local_s, far_s
 ):
     pairs = []
     core = lax.axis_index("inner") % 2
-    for w, (holder, place) in enumerate(((1, 0), (0, 0), (0, 2), (1, 2))):
+    for w, (holder, place) in enumerate(((1, 2), (0, 2), (0, 0), (1, 0))):
         both = spread(came_ref[holder, place + core])
         for side in (0, 1):
             slot = 2 * w + side
@@ -198,16 +212,16 @@
     sources = split(jnp.concatenate(sources, axis=0))
     far = dot3k((second_ref[0:64], second_ref[64:128]), sources)
     first = lanes((16, 128)) < 64
-    local = []
     for t in range(4):
-        parts = []
         for h in range(2):
             a = total_s[h, pl.ds(2 * t, 16, stride=8), :]
             b = total_s[h, pl.ds(2 * t + 1, 16, stride=8), :]
-            parts.append(jnp.where(first, a, pltpu.roll(b, 64, 1)))
-            parts.append(jnp.where(first, pltpu.roll(a, 64, 1), b))
-        local.append(jnp.concatenate(parts, axis=0))
-    local = jnp.concatenate(local, axis=1)
+            local_s[t, pl.ds(2 * h, 16, stride=4), :] = jnp.where(first, a, pltpu.roll(b, 64, 1))
+            local_s[t, pl.ds(2 * h + 1, 16, stride=4), :] = jnp.where(first, pltpu.roll(a, 64, 1), b)
+    local = jnp.concatenate([local_s[t] for t in range(4)], axis=1)
+    for c in range(4):
+        far_s[pl.ds(c, 16, stride=4), :] = far[16 * c : 16 * c + 16]
+    far = far_s[...]
     operators = split(l2l_ref[...].reshape(512, 64))
     lowered = dot3k(operators, split(far))
     first = lanes((64, 128)) < 64
@@ -229,26 +243,34 @@
     return pltpu.with_memory_space_constraint(x, pltpu.HBM)
 
 
-def upward(leaf_multipoles, m2m_ops, send_blocks, send_counts):
+def upward(leaf_multipoles, m2m_ops, m2l_ops, send_blocks, send_counts, list1_src, list1_pat, list2_src, list2_pat):
+    patterns = m2l_ops.shape[0]
+    lists = [x[0, 0] for x in (list1_src, list1_pat, list2_src, list2_pat)]
     return pl.pallas_call(
         upward_kernel,
         out_shape=[
             jax.ShapeDtypeStruct((64, 512), F32),
             jax.ShapeDtypeStruct((4, 64, 128), F32),
-            jax.ShapeDtypeStruct((8, 32, 128), F32),
+            pltpu.HBM((8, 32, 128), F32),
+            jax.ShapeDtypeStruct((144, patterns), BF16),
+            jax.ShapeDtypeStruct((EARLY, 128, 256), F32),
+            jax.ShapeDtypeStruct((2, 16 * EARLY, 128), F32),
         ],
-        in_specs=[HBM] * 4,
-        out_specs=[VMEM] * 3,
+        in_specs=[HBM] * 9,
+        out_specs=[VMEM, VMEM, HBM, VMEM, VMEM, VMEM],
         scratch_shapes=[
             pltpu.SMEM((1, 1, 2, 4), jnp.int32),
             pltpu.SMEM((1, 1, 4), jnp.int32),
             pltpu.VMEM((8, 64, 512), F32),
             pltpu.VMEM((8, 64, 64), F32),
+            *[pltpu.VMEM(x.shape, jnp.int32) for x in lists],
+            pltpu.VMEM((4 * EARLY, 64, patterns), F32),
             pltpu.VMEM((64, 512), F32),
             pltpu.VMEM((512, 128), F32),
             pltpu.VMEM((64, 512), F32),
             pltpu.VMEM((8, 64, 128), F32),
-            pltpu.SemaphoreType.DMA((5,)),
+            pltpu.VMEM((8, 32, 128), F32),
+            pltpu.SemaphoreType.DMA((11,)),
         ],
         compiler_params=LIMIT,
         cost_estimate=pl.CostEstimate(flops=10**9, bytes_accessed=12 * 10**6, transcendentals=0),
@@ -258,10 +280,12 @@
         in_hbm(send_counts),
         in_hbm(leaf_multipoles),
         in_hbm(m2m_ops),
+        *[in_hbm(x) for x in lists],
+        in_hbm(jnp.transpose(m2l_ops, (1, 2, 0))),
     )
 
 
-def weights(list1_src, list1_pat, list2_src, list2_pat, m2l_ops, level1):
+def weights(picks, table, early, m2l_ops, level1):
     patterns = m2l_ops.shape[0]
     return pl.pallas_call(
         weights_kernel,
@@ -271,24 +295,17 @@
             jax.ShapeDtypeStruct((128, 256), F32),
             jax.ShapeDtypeStruct((128, 1024), BF16),
         ],
-        in_specs=[VMEM] * 4 + [HBM] + [VMEM],
+        in_specs=[VMEM] * 3 + [HBM] + [VMEM],
         out_specs=[VMEM] * 4,
         scratch_shapes=[
-            pltpu.VMEM((16, 128, 256), F32),
-            pltpu.VMEM((2, 256, 128), F32),
-            pltpu.VMEM((64, 64, patterns), F32),
-            pltpu.SemaphoreType.DMA((16,)),
+            pltpu.VMEM((16 - EARLY, 128, 256), F32),
+            pltpu.VMEM((2, 256 - 16 * EARLY, 128), F32),
+            pltpu.VMEM((64 - 4 * EARLY, 64, patterns), F32),
+            pltpu.SemaphoreType.DMA,
         ],
         compiler_params=LIMIT,
         name="weights",
-    )(
-        list1_src[0, 0],
-        list1_pat[0, 0],
-        list2_src[0, 0],
-        list2_pat[0, 0],
-        in_hbm(jnp.transpose(m2l_ops, (1, 2, 0))),
-        level1,
-    )
+    )(picks, table, early, in_hbm(jnp.transpose(m2l_ops, (1, 2, 0))), level1)
 
 
 def downward(high, low, own, second, came, l2l_ops):
@@ -297,7 +314,7 @@
         out_shape=jax.ShapeDtypeStruct((8, 64, 512), F32),
         in_specs=[VMEM] * 6,
         out_specs=VMEM,
-        scratch_shapes=[pltpu.VMEM((2, 128, 128), F32)],
+        scratch_shapes=[pltpu.VMEM((2, 128, 128), F32), pltpu.VMEM((4, 64, 128), F32), pltpu.VMEM((64, 128), F32)],
         compiler_params=LIMIT,
         name="downward",
     )(high, low, own, second, came, l2l_ops)
@@ -307,7 +324,9 @@
     leaf_multipoles, m2m_ops, l2l_ops, m2l_ops, send_blocks, send_counts, list1_src, list1_pat, list2_src, list2_pat
 ):
     doms, inners = lax.axis_size("dom"), lax.axis_size("inner")
-    level1, sends, level2 = upward(leaf_multipoles, m2m_ops, send_blocks, send_counts)
+    level1, sends, level2, picks, table, early = upward(
+        leaf_multipoles, m2m_ops, m2l_ops, send_blocks, send_counts, list1_src, list1_pat, list2_src, list2_pat
+    )
     core = lax.axis_index("inner") % 2
     cores = [[2 * x, 2 * x + 1] for x in range(inners // 2)]
 
@@ -330,8 +349,8 @@
     lower = lax.dynamic_index_in_dim(chip_sends, 1 - core, 1, keepdims=False)
     came_up = routed(upper, 1)
     came_down = routed(lower, -1)
-    operators = weights(list1_src, list1_pat, list2_src, list2_pat, m2l_ops, level1)
-    came = jnp.concatenate([came_up, came_down, own_side.reshape(4, 64, 128)], axis=0)
+    operators = weights(picks, table, early, m2l_ops, level1)
+    came = jnp.concatenate([came_down, came_up, own_side.reshape(4, 64, 128)], axis=0)
     return downward(*operators, both_cores(came), l2l_ops)
 
 

time: 35.4 us -> 36.2 us (1.023)
  waiting for transfers between devices: 0.01 us -> 1.32 us
  Pallas kernels: 10.2 us -> 9.58 us
    pallas_call x1, Pallas kernels: 4.82 us -> 3.39 us  [weights(): pl.pallas_call(weights_kernel, out_shape=[jax.ShapeDtypeStruct((8, 128, 2...]
    ppermute x2, waiting for transfers between devices: 0.01 us -> 1.32 us  [routed(): return lax.ppermute(block, ('dom', 'inner'), route)]
    pallas_call x1, Pallas kernels: 2.83 us -> 3.59 us  [upward(): pl.pallas_call(upward_kernel, out_shape=[jax.ShapeDtypeStruct((64, 512),...]
  transfers between devices with their start and end apart: 3 -> 3, of which waited for: 0 -> 1; matrix products, arithmetic and copies ran while one was open for 0% -> 0% of each run, Pallas kernels for 14% -> 9%
where the time goes in v4:
time: 36.2 us; the launch traced here: 35.9 us
  blocking collectives  14.9 us (41%)
  starting transfers between devices  10 us (28%)
  Pallas kernels  9.58 us (26%)
  waiting for transfers between devices  1.32 us (4%)
    all_gather x2, blocking collectives, both_cores(): return lax.all_gather(block, 'inner', axis=0, axis_index_groups=cores)  14.9 us
    all_to_all x1, starting transfers between devices, on_device(): own_side = lax.all_to_all(level2, 'inner', 0, 0, axis_index_groups=chips)  7.45 us
    pallas_call x1, Pallas kernels, upward(): pl.pallas_call(upward_kernel, out_shape=[jax.ShapeDtypeStruct((64, 512),...  3.59 us
    pallas_call x1, Pallas kernels, weights(): pl.pallas_call(weights_kernel, out_shape=[jax.ShapeDtypeStruct((8, 128, 2...  3.39 us
    pallas_call x1, Pallas kernels, downward(): pl.pallas_call(downward_kernel, out_shape=jax.ShapeDtypeStruct((8, 64, 51...  2.6 us
    ppermute x2, starting transfers between devices, routed(): return lax.ppermute(block, ('dom', 'inner'), route)  2.59 us
    ppermute x2, waiting for transfers between devices, routed(): return lax.ppermute(block, ('dom', 'inner'), route)  1.32 us
  transfers between devices with their start and end apart: 3, of which 1 were waited for; matrix products, arithmetic and copies ran while one was open for 0% of the time, Pallas kernels for 9%

profile of v4, /device:TPU:1, one launch (start us, length us, event | category | flops | bytes accessed | tf_op | source)
XLA Modules:
  0.0 35.9 jit_solution(7763925442851067644)
XLA Ops:
  0.0 3.6 %upward.1 = (f32[64,512]{1,0:T(8,128)S(1)}, f32[4,64,128]{2,1,0:T(8,128)S(1)}, f32[8,32,128]{2,1,0:T(8,128)}, bf16[144,189]{1,0:T(8,128)(2,1)S(1)}, f32[8,128,25...) custom-call(s32[1,1,2,4]{3,2,1,0:T(2,128)} %bitcast.20, s32[1,1,4]{2,1,0:T(1,128)} %counts_hbm.1, f32[8,64,512]{2,1,0:T(8,128)} %leaf_hbm.1, ...), custom_call_target="tpu_custom_call" | custom-call | flops 1000000000 | bytes 12000000 | tf_op jit(solution)/shard_map/upward/pallas_call | solution.py:249
  3.6 0.0 copy-start
  3.6 7.5 %all-to-all-start = ((f32[8,32,128]{2,1,0:T(8,128)}), f32[8,32,128]{2,1,0:T(8,128)S(1)}, u32[]{:S(2)}, u32[]{:S(2)}) async-start(f32[8,32,128]{2,1,0:T(8,128)} %get-tuple-element.24), calls=%async_computation | async-start | bytes 262144 | tf_op jit(solution)/shard_map/all_to_all | solution.py:346
  11.1 11.9 %all-gather = f32[8,64,128]{2,1,0:T(8,128)S(1)} all-gather(f32[4,64,128]{2,1,0:T(8,128)S(1)} %get-tuple-element.23), channel_id=2, replica_groups={{0,1},{2,3},{4,5},{6,7},{8,9},{10,11},{12,13},{14,15},{16,17},{18,19},{..., dimensions={0}, use_global_device_ids=true | all-gather | bytes 393216 | tf_op jit(solution)/shard_map/all_gather | solution.py:343
  23.0 1.3 %collective-permute-start.1 = (f32[2,64,128]{2,1,0:T(8,128)S(1)}, f32[2,64,128]{2,1,0:T(8,128)S(1)}, u32[]{:S(2)}, u32[]{:S(2)}) collective-permute-start(f32[2,64,128]{2,1,0:T(8,128)S(1)} %get-tuple-element.26), channel_id=1, source_target_pairs={{0,16},{1,33},{2,18},{3,35},{4,20},{5,37},{6,22},{7,39},{8,24},{9,... | collective-permute-start | bytes 196616 | tf_op jit(solution)/shard_map/ppermute | solution.py:340
  24.3 1.3 %collective-permute-start = (f32[2,64,128]{2,1,0:T(8,128)S(1)}, f32[2,64,128]{2,1,0:T(8,128)S(1)}, u32[]{:S(2)}, u32[]{:S(2)}) collective-permute-start(f32[2,64,128]{2,1,0:T(8,128)S(1)} %get-tuple-element.25), channel_id=1, source_target_pairs={{16,0},{18,2},{20,4},{22,6},{24,8},{26,10},{28,12},{30,14},{32,16}... | collective-permute-start | bytes 196616 | tf_op jit(solution)/shard_map/ppermute | solution.py:340
  25.6 3.4 %weights.1 = (bf16[8,128,256]{2,1,0:T(8,128)(2,1)S(1)}, bf16[8,128,256]{2,1,0:T(8,128)(2,1)S(1)}, f32[128,256]{1,0:T(8,128)S(1)}, bf16[128,1024]{1,0:T(8,128)(2,1)S(1)}) custom-call(bf16[144,189]{1,0:T(8,128)(2,1)S(1)} %get-tuple-element.15.picks_ref, f32[8,128,256]{2,1,0:T(8,128)S(1)} %get-tuple-element.16.table_ref, ...), custom_call_target="tpu_custom_call" | custom-call | tf_op jit(solution)/shard_map/weights/pallas_call | solution.py:290
  28.9 0.0 collective-permute-done.1
  29.0 1.3 %collective-permute-done = f32[2,64,128]{2,1,0:T(8,128)S(1)} collective-permute-done((f32[2,64,128]{2,1,0:T(8,128)S(1)}, f32[2,64,128]{2,1,0:T(8,128)S(1)}, u32[]{:S(2)}, u32[]{:S(2)}) %collective-permute-start) | collective-permute-done | bytes 65568 | tf_op jit(solution)/shard_map/ppermute | solution.py:340
  30.3 0.0 all-to-all-done
  30.3 3.0 %all-gather.1 = f32[16,64,128]{2,1,0:T(8,128)S(1)} all-gather(f32[8,64,128]{2,1,0:T(8,128)S(1)} %pad_maximum_fusion), channel_id=3, replica_groups={{0,1},{2,3},{4,5},{6,7},{8,9},{10,11},{12,13},{14,15},{16,17},{18,19},{..., dimensions={0}, use_global_device_ids=true | all-gather | bytes 786432 | tf_op jit(solution)/shard_map/all_gather | solution.py:343
  33.3 0.0 copy-done
  33.3 2.6 %downward.1 = f32[8,64,512]{2,1,0:T(8,128)} custom-call(bf16[8,128,256]{2,1,0:T(8,128)(2,1)S(1)} %get-tuple-element.19.high_ref, bf16[8,128,256]{2,1,0:T(8,128)(2,1)S(1)} %get-tuple-element.20.low_ref, f32[128,256]{1,0:T(8,128)S(1)} %get-tuple-element.21.own_ref, bf16[128,1024]{1,0:T(8,128)(2,1)S(1)} %get-tuple-element.22.second_ref, ...), custom_call_target="tpu_custom_call" | custom-call | tf_op jit(solution)/shard_map/downward/pallas_call | solution.py:312
  (2 shorter events, 0.0 us)
Async XLA Ops:
  3.6 29.7 %copy-start = (f32[8,64,64]{2,1,0:T(8,128)S(1)}, f32[8,64,64]{2,1,0:T(8,128)}, u32[]{:S(2)}) copy-start(f32[8,64,64]{2,1,0:T(8,128)} %l2l_ref.1) | copy-start | bytes 393220
  3.6 26.7 %all-to-all-start = ((f32[8,32,128]{2,1,0:T(8,128)}), f32[8,32,128]{2,1,0:T(8,128)S(1)}, u32[]{:S(2)}, u32[]{:S(2)}) async-start(f32[8,32,128]{2,1,0:T(8,128)} %get-tuple-element.24), calls=%async_computation | async-start | bytes 262144 | tf_op jit(solution)/shard_map/all_to_all | solution.py:346
  23.0 6.0 %collective-permute-start.1 = (f32[2,64,128]{2,1,0:T(8,128)S(1)}, f32[2,64,128]{2,1,0:T(8,128)S(1)}, u32[]{:S(2)}, u32[]{:S(2)}) collective-permute-start(f32[2,64,128]{2,1,0:T(8,128)S(1)} %get-tuple-element.26), channel_id=1, source_target_pairs={{0,16},{1,33},{2,18},{3,35},{4,20},{5,37},{6,22},{7,39},{8,24},{9,... | collective-permute-start | bytes 196616 | tf_op jit(solution)/shard_map/ppermute | solution.py:340
  24.3 6.0 %collective-permute-start = (f32[2,64,128]{2,1,0:T(8,128)S(1)}, f32[2,64,128]{2,1,0:T(8,128)S(1)}, u32[]{:S(2)}, u32[]{:S(2)}) collective-permute-start(f32[2,64,128]{2,1,0:T(8,128)S(1)} %get-tuple-element.25), channel_id=1, source_target_pairs={{16,0},{18,2},{20,4},{22,6},{24,8},{26,10},{28,12},{30,14},{32,16}... | collective-permute-start | bytes 196616 | tf_op jit(solution)/shard_map/ppermute | solution.py:340

commit v5 on v4

--- a/solution.py
+++ b/solution.py
@@ -66,7 +66,7 @@
     return result
 
 
-EARLY = 8
+EARLY = 4
 
 
 def translate(picks, m2l_ref, table_ref, second_ref):
@@ -193,8 +193,11 @@
 ):
     pairs = []
     core = lax.axis_index("inner") % 2
-    for w, (holder, place) in enumerate(((1, 2), (0, 2), (0, 0), (1, 0))):
-        both = spread(came_ref[holder, place + core])
+    dom = lax.axis_index("dom")
+    for w, (holder, above) in enumerate(((1, 0), (0, 0), (0, 1), (1, 1))):
+        first_up = 1 - (dom >> holder) % 2
+        phase = (first_up + above) % 2
+        both = spread(came_ref[holder, 2 * phase + core])
         for side in (0, 1):
             slot = 2 * w + side
             pairs.append(((high_ref[slot], low_ref[slot]), both[side]))
@@ -330,11 +333,14 @@
     core = lax.axis_index("inner") % 2
     cores = [[2 * x, 2 * x + 1] for x in range(inners // 2)]
 
-    def routed(block, side):
+    first_up = (lax.axis_index("dom") >> core) % 2 == 0
+
+    def swapped(block, phase):
         route = []
         for d in range(doms):
             for i in range(inners):
-                to = d + side * (1 + i % 2)
+                away = 1 + i % 2
+                to = d + away if d // away % 2 == phase else d - away
                 if 0 <= to < doms:
                     route.append((d * inners + i, to * inners + i))
         return lax.ppermute(block, ("dom", "inner"), route)
@@ -345,12 +351,13 @@
     chips = [[2 * x + c for x in range(inners // 2)] for c in range(2)]
     own_side = lax.all_to_all(level2, "inner", 0, 0, axis_index_groups=chips)
     chip_sends = both_cores(sends)
-    upper = lax.dynamic_index_in_dim(chip_sends, 2 + core, 1, keepdims=False)
-    lower = lax.dynamic_index_in_dim(chip_sends, 1 - core, 1, keepdims=False)
-    came_up = routed(upper, 1)
-    came_down = routed(lower, -1)
+    to_up, to_down = 2 + core, 1 - core
+    first = lax.dynamic_index_in_dim(chip_sends, jnp.where(first_up, to_up, to_down), 1, keepdims=False)
+    second = lax.dynamic_index_in_dim(chip_sends, jnp.where(first_up, to_down, to_up), 1, keepdims=False)
+    came_first = swapped(first, 0)
+    came_second = swapped(second, 1)
     operators = weights(picks, table, early, m2l_ops, level1)
-    came = jnp.concatenate([came_down, came_up, own_side.reshape(4, 64, 128)], axis=0)
+    came = jnp.concatenate([came_first, came_second, own_side.reshape(4, 64, 128)], axis=0)
     return downward(*operators, both_cores(came), l2l_ops)
 
 

time: 36.2 us -> 36.2 us (level)
  the two profiles are of different devices: /device:TPU:1 before, /device:TPU:35 now
where the time goes in v5:
time: 36.2 us; the launch traced here: 35.9 us
  starting transfers between devices  19.7 us (54%)
  Pallas kernels  10 us (28%)
  blocking collectives  5.03 us (14%)
  waiting for transfers between devices  1.06 us (3%)
    ppermute x2, starting transfers between devices, swapped(): return lax.ppermute(block, ('dom', 'inner'), route)  12.8 us
    all_to_all x1, starting transfers between devices, on_device(): own_side = lax.all_to_all(level2, 'inner', 0, 0, axis_index_groups=chips)  6.88 us
    all_gather x2, blocking collectives, both_cores(): return lax.all_gather(block, 'inner', axis=0, axis_index_groups=cores)  5.03 us
    pallas_call x1, Pallas kernels, weights(): pl.pallas_call(weights_kernel, out_shape=[jax.ShapeDtypeStruct((8, 128, 2...  4.11 us
    pallas_call x1, Pallas kernels, upward(): pl.pallas_call(upward_kernel, out_shape=[jax.ShapeDtypeStruct((64, 512),...  3.34 us
    pallas_call x1, Pallas kernels, downward(): pl.pallas_call(downward_kernel, out_shape=jax.ShapeDtypeStruct((8, 64, 51...  2.59 us
    ppermute x2, waiting for transfers between devices, swapped(): return lax.ppermute(block, ('dom', 'inner'), route)  1.06 us
  transfers between devices with their start and end apart: 3, of which 1 were waited for; matrix products, arithmetic and copies ran while one was open for 0% of the time, Pallas kernels for 11%

profile of v5, /device:TPU:35, one launch (start us, length us, event | category | flops | bytes accessed | tf_op | source)
XLA Modules:
  0.0 35.9 jit_solution(17889913127349277991)
XLA Ops:
  0.0 3.3 %upward.1 = (f32[64,512]{1,0:T(8,128)S(1)}, f32[4,64,128]{2,1,0:T(8,128)S(1)}, f32[8,32,128]{2,1,0:T(8,128)}, bf16[144,189]{1,0:T(8,128)(2,1)S(1)}, f32[4,128,25...) custom-call(s32[1,1,2,4]{3,2,1,0:T(2,128)} %bitcast.20, s32[1,1,4]{2,1,0:T(1,128)} %counts_hbm.1, f32[8,64,512]{2,1,0:T(8,128)} %leaf_hbm.1, ...), custom_call_target="tpu_custom_call" | custom-call | flops 1000000000 | bytes 12000000 | tf_op jit(solution)/shard_map/upward/pallas_call | solution.py:252
  3.3 0.0 copy-start
  3.4 6.9 %all-to-all-start = ((f32[8,32,128]{2,1,0:T(8,128)}), f32[8,32,128]{2,1,0:T(8,128)S(1)}, u32[]{:S(2)}, u32[]{:S(2)}) async-start(f32[8,32,128]{2,1,0:T(8,128)} %get-tuple-element.24), calls=%async_computation | async-start | bytes 262144 | tf_op jit(solution)/shard_map/all_to_all | solution.py:352
  10.2 2.9 %all-gather = f32[8,64,128]{2,1,0:T(8,128)S(1)} all-gather(f32[4,64,128]{2,1,0:T(8,128)S(1)} %get-tuple-element.23), channel_id=2, replica_groups={{0,1},{2,3},{4,5},{6,7},{8,9},{10,11},{12,13},{14,15},{16,17},{18,19},{..., dimensions={0}, use_global_device_ids=true | all-gather | bytes 393216 | tf_op jit(solution)/shard_map/all_gather | solution.py:349
  13.1 10.9 %collective-permute-start = (f32[2,64,128]{2,1,0:T(8,128)S(1)}, f32[2,64,128]{2,1,0:T(8,128)S(1)}, u32[]{:S(2)}, u32[]{:S(2)}) collective-permute-start(f32[2,64,128]{2,1,0:T(8,128)S(1)} %get-tuple-element.25), channel_id=1, source_target_pairs={{0,16},{1,33},{2,18},{3,35},{4,20},{5,37},{6,22},{7,39},{8,24},{9,... | collective-permute-start | bytes 196616 | tf_op jit(solution)/shard_map/ppermute | solution.py:346
  24.0 1.9 %collective-permute-start.1 = (f32[2,64,128]{2,1,0:T(8,128)S(1)}, f32[2,64,128]{2,1,0:T(8,128)S(1)}, u32[]{:S(2)}, u32[]{:S(2)}) collective-permute-start(f32[2,64,128]{2,1,0:T(8,128)S(1)} %get-tuple-element.26), channel_id=1, source_target_pairs={{16,32},{18,34},{20,36},{22,38},{24,40},{26,42},{28,44},{30,46},{3... | collective-permute-start | bytes 196616 | tf_op jit(solution)/shard_map/ppermute | solution.py:346
  25.9 4.1 %weights.1 = (bf16[8,128,256]{2,1,0:T(8,128)(2,1)S(1)}, bf16[8,128,256]{2,1,0:T(8,128)(2,1)S(1)}, f32[128,256]{1,0:T(8,128)S(1)}, bf16[128,1024]{1,0:T(8,128)(2,1)S(1)}) custom-call(bf16[144,189]{1,0:T(8,128)(2,1)S(1)} %get-tuple-element.15.picks_ref, f32[4,128,256]{2,1,0:T(8,128)S(1)} %get-tuple-element.16.table_ref, ...), custom_call_target="tpu_custom_call" | custom-call | tf_op jit(solution)/shard_map/weights/pallas_call | solution.py:293
  30.1 0.0 collective-permute-done
  30.1 1.1 %collective-permute-done.1 = f32[2,64,128]{2,1,0:T(8,128)S(1)} collective-permute-done((f32[2,64,128]{2,1,0:T(8,128)S(1)}, f32[2,64,128]{2,1,0:T(8,128)S(1)}, u32[]{:S(2)}, u32[]{:S(2)}) %collective-permute-start.1) | collective-permute-done | bytes 65568 | tf_op jit(solution)/shard_map/ppermute | solution.py:346
  31.1 0.0 all-to-all-done
  31.2 2.2 %all-gather.1 = f32[16,64,128]{2,1,0:T(8,128)S(1)} all-gather(f32[8,64,128]{2,1,0:T(8,128)S(1)} %pad_maximum_fusion), channel_id=3, replica_groups={{0,1},{2,3},{4,5},{6,7},{8,9},{10,11},{12,13},{14,15},{16,17},{18,19},{..., dimensions={0}, use_global_device_ids=true | all-gather | bytes 786432 | tf_op jit(solution)/shard_map/all_gather | solution.py:349
  33.3 0.0 copy-done
  33.3 2.6 %downward.1 = f32[8,64,512]{2,1,0:T(8,128)} custom-call(bf16[8,128,256]{2,1,0:T(8,128)(2,1)S(1)} %get-tuple-element.19.high_ref, bf16[8,128,256]{2,1,0:T(8,128)(2,1)S(1)} %get-tuple-element.20.low_ref, f32[128,256]{1,0:T(8,128)S(1)} %get-tuple-element.21.own_ref, bf16[128,1024]{1,0:T(8,128)(2,1)S(1)} %get-tuple-element.22.second_ref, ...), custom_call_target="tpu_custom_call" | custom-call | tf_op jit(solution)/shard_map/downward/pallas_call | solution.py:315
  (2 shorter events, 0.0 us)
Async XLA Ops:
  3.3 30.0 %copy-start = (f32[8,64,64]{2,1,0:T(8,128)S(1)}, f32[8,64,64]{2,1,0:T(8,128)}, u32[]{:S(2)}) copy-start(f32[8,64,64]{2,1,0:T(8,128)} %l2l_ref.1) | copy-start | bytes 393220
  3.4 27.8 %all-to-all-start = ((f32[8,32,128]{2,1,0:T(8,128)}), f32[8,32,128]{2,1,0:T(8,128)S(1)}, u32[]{:S(2)}, u32[]{:S(2)}) async-start(f32[8,32,128]{2,1,0:T(8,128)} %get-tuple-element.24), calls=%async_computation | async-start | bytes 262144 | tf_op jit(solution)/shard_map/all_to_all | solution.py:352
  13.1 17.0 %collective-permute-start = (f32[2,64,128]{2,1,0:T(8,128)S(1)}, f32[2,64,128]{2,1,0:T(8,128)S(1)}, u32[]{:S(2)}, u32[]{:S(2)}) collective-permute-start(f32[2,64,128]{2,1,0:T(8,128)S(1)} %get-tuple-element.25), channel_id=1, source_target_pairs={{0,16},{1,33},{2,18},{3,35},{4,20},{5,37},{6,22},{7,39},{8,24},{9,... | collective-permute-start | bytes 196616 | tf_op jit(solution)/shard_map/ppermute | solution.py:346
  24.0 7.1 %collective-permute-start.1 = (f32[2,64,128]{2,1,0:T(8,128)S(1)}, f32[2,64,128]{2,1,0:T(8,128)S(1)}, u32[]{:S(2)}, u32[]{:S(2)}) collective-permute-start(f32[2,64,128]{2,1,0:T(8,128)S(1)} %get-tuple-element.26), channel_id=1, source_target_pairs={{16,32},{18,34},{20,36},{22,38},{24,40},{26,42},{28,44},{30,46},{3... | collective-permute-start | bytes 196616 | tf_op jit(solution)/shard_map/ppermute | solution.py:346

commit v6 on v3

--- a/solution.py
+++ b/solution.py
@@ -179,8 +179,11 @@
 ):
     pairs = []
     core = lax.axis_index("inner") % 2
-    for w, (holder, place) in enumerate(((1, 0), (0, 0), (0, 2), (1, 2))):
-        both = spread(came_ref[holder, place + core])
+    dom = lax.axis_index("dom")
+    for w, (holder, above) in enumerate(((1, 0), (0, 0), (0, 1), (1, 1))):
+        first_up = 1 - (dom >> holder) % 2
+        phase = (first_up + above) % 2
+        both = spread(came_ref[holder, 2 * (1 - phase) + core])
         for side in (0, 1):
             slot = 2 * w + side
             pairs.append(((high_ref[slot], low_ref[slot]), both[side]))
@@ -311,11 +314,14 @@
     core = lax.axis_index("inner") % 2
     cores = [[2 * x, 2 * x + 1] for x in range(inners // 2)]
 
-    def routed(block, side):
+    first_up = (lax.axis_index("dom") >> core) % 2 == 0
+
+    def swapped(block, phase):
         route = []
         for d in range(doms):
             for i in range(inners):
-                to = d + side * (1 + i % 2)
+                away = 1 + i % 2
+                to = d + away if d // away % 2 == phase else d - away
                 if 0 <= to < doms:
                     route.append((d * inners + i, to * inners + i))
         return lax.ppermute(block, ("dom", "inner"), route)
@@ -326,12 +332,13 @@
     chips = [[2 * x + c for x in range(inners // 2)] for c in range(2)]
     own_side = lax.all_to_all(level2, "inner", 0, 0, axis_index_groups=chips)
     chip_sends = both_cores(sends)
-    upper = lax.dynamic_index_in_dim(chip_sends, 2 + core, 1, keepdims=False)
-    lower = lax.dynamic_index_in_dim(chip_sends, 1 - core, 1, keepdims=False)
-    came_up = routed(upper, 1)
-    came_down = routed(lower, -1)
+    to_up, to_down = 2 + core, 1 - core
+    first = lax.dynamic_index_in_dim(chip_sends, jnp.where(first_up, to_up, to_down), 1, keepdims=False)
+    second = lax.dynamic_index_in_dim(chip_sends, jnp.where(first_up, to_down, to_up), 1, keepdims=False)
+    came_first = swapped(first, 0)
+    came_second = swapped(second, 1)
     operators = weights(list1_src, list1_pat, list2_src, list2_pat, m2l_ops, level1)
-    came = jnp.concatenate([came_up, came_down, own_side.reshape(4, 64, 128)], axis=0)
+    came = jnp.concatenate([came_second, came_first, own_side.reshape(4, 64, 128)], axis=0)
     return downward(*operators, both_cores(came), l2l_ops)
 
 

time: 35.4 us -> 34.8 us (0.983)
  blocking collectives: 14.7 us -> 14.1 us
    all_gather x2, blocking collectives: 14.7 us -> 14.1 us  [both_cores(): return lax.all_gather(block, 'inner', axis=0, axis_index_groups=cores)]
where the time goes in v6:
time: 34.8 us; the launch traced here: 34.5 us
  blocking collectives  14.1 us (41%)
  Pallas kernels  10.2 us (29%)
  starting transfers between devices  10 us (29%)
    all_gather x2, blocking collectives, both_cores(): return lax.all_gather(block, 'inner', axis=0, axis_index_groups=cores)  14.1 us
    all_to_all x1, starting transfers between devices, on_device(): own_side = lax.all_to_all(level2, 'inner', 0, 0, axis_index_groups=chips)  7.45 us
    pallas_call x1, Pallas kernels, weights(): pl.pallas_call(weights_kernel, out_shape=[jax.ShapeDtypeStruct((8, 128, 2...  4.82 us
    pallas_call x1, Pallas kernels, upward(): pl.pallas_call(upward_kernel, out_shape=[jax.ShapeDtypeStruct((64, 512),...  2.83 us
    ppermute x2, starting transfers between devices, swapped(): return lax.ppermute(block, ('dom', 'inner'), route)  2.59 us
    pallas_call x1, Pallas kernels, downward(): pl.pallas_call(downward_kernel, out_shape=jax.ShapeDtypeStruct((8, 64, 51...  2.57 us
  transfers between devices with their start and end apart: 3, of which 0 were waited for; matrix products, arithmetic and copies ran while one was open for 0% of the time, Pallas kernels for 14%

profile of v6, /device:TPU:1, one launch (start us, length us, event | category | flops | bytes accessed | tf_op | source)
XLA Modules:
  0.0 34.5 jit_solution(13988561563951220023)
XLA Ops:
  0.0 0.0 copy-start.4
  0.0 0.0 copy-start.3
  0.0 0.0 copy-start.2
  0.0 0.0 copy-start.1
  0.0 2.8 %upward.1 = (f32[64,512]{1,0:T(8,128)S(1)}, f32[4,64,128]{2,1,0:T(8,128)S(1)}, f32[8,32,128]{2,1,0:T(8,128)}) custom-call(s32[1,1,2,4]{3,2,1,0:T(2,128)} %bitcast.21, s32[1,1,4]{2,1,0:T(1,128)} %counts_hbm.1, f32[8,64,512]{2,1,0:T(8,128)} %leaf_hbm.1, f32[8,64,64]{2,1,0:T(8,128)} %m2m_hbm.1), custom_call_target="tpu_custom_call" | custom-call | flops 1000000000 | bytes 12000000 | tf_op jit(solution)/shard_map/upward/pallas_call | solution.py:236
  2.9 0.0 copy-start
  2.9 7.5 %all-to-all-start = ((f32[8,32,128]{2,1,0:T(8,128)}), f32[8,32,128]{2,1,0:T(8,128)S(1)}, u32[]{:S(2)}, u32[]{:S(2)}) async-start(f32[8,32,128]{2,1,0:T(8,128)} %get-tuple-element.18), calls=%async_computation | async-start | bytes 262144 | tf_op jit(solution)/shard_map/all_to_all | solution.py:333
  10.3 11.9 %all-gather = f32[8,64,128]{2,1,0:T(8,128)S(1)} all-gather(f32[4,64,128]{2,1,0:T(8,128)S(1)} %get-tuple-element.17), channel_id=2, replica_groups={{0,1},{2,3},{4,5},{6,7},{8,9},{10,11},{12,13},{14,15},{16,17},{18,19},{..., dimensions={0}, use_global_device_ids=true | all-gather | bytes 393216 | tf_op jit(solution)/shard_map/all_gather | solution.py:330
  22.2 0.7 %collective-permute-start = (f32[2,64,128]{2,1,0:T(8,128)S(1)}, f32[2,64,128]{2,1,0:T(8,128)S(1)}, u32[]{:S(2)}, u32[]{:S(2)}) collective-permute-start(f32[2,64,128]{2,1,0:T(8,128)S(1)} %get-tuple-element.19), channel_id=1, source_target_pairs={{16,32},{18,34},{20,36},{22,38},{24,40},{26,42},{28,44},{30,46},{3... | collective-permute-start | bytes 196616 | tf_op jit(solution)/shard_map/ppermute | solution.py:327
  22.9 1.9 %collective-permute-start.1 = (f32[2,64,128]{2,1,0:T(8,128)S(1)}, f32[2,64,128]{2,1,0:T(8,128)S(1)}, u32[]{:S(2)}, u32[]{:S(2)}) collective-permute-start(f32[2,64,128]{2,1,0:T(8,128)S(1)} %get-tuple-element.20), channel_id=1, source_target_pairs={{0,16},{1,33},{2,18},{3,35},{4,20},{5,37},{6,22},{7,39},{8,24},{9,... | collective-permute-start | bytes 196616 | tf_op jit(solution)/shard_map/ppermute | solution.py:327
  24.8 0.0 copy-done.4
  24.8 0.0 copy-done.3
  24.9 0.0 copy-done.2
  24.9 0.0 copy-done.1
  24.9 4.8 %weights.1 = (bf16[8,128,256]{2,1,0:T(8,128)(2,1)S(1)}, bf16[8,128,256]{2,1,0:T(8,128)(2,1)S(1)}, f32[128,256]{1,0:T(8,128)S(1)}, bf16[128,1024]{1,0:T(8,128)(2,1)S(1)}) custom-call(s32[8,120]{1,0:T(8,128)S(1)} %bitcast.14, s32[8,120]{1,0:T(8,128)S(1)} %bitcast.15, s32[1,8]{1,0:T(1,128)S(1)} %bitcast.16, s32[1,8]{1,0:T(1,128)S(1)} %bitcast.17, ...), custom_call_target="tpu_custom_call" | custom-call | tf_op jit(solution)/shard_map/weights/pallas_call | solution.py:269
  29.7 0.0 collective-permute-done
  29.7 0.0 collective-permute-done.1
  29.7 0.0 all-to-all-done
  29.8 2.2 %all-gather.1 = f32[16,64,128]{2,1,0:T(8,128)S(1)} all-gather(f32[8,64,128]{2,1,0:T(8,128)S(1)} %pad_maximum_fusion), channel_id=3, replica_groups={{0,1},{2,3},{4,5},{6,7},{8,9},{10,11},{12,13},{14,15},{16,17},{18,19},{..., dimensions={0}, use_global_device_ids=true | all-gather | bytes 786432 | tf_op jit(solution)/shard_map/all_gather | solution.py:330
  32.0 0.0 copy-done
  32.0 2.6 %downward.1 = f32[8,64,512]{2,1,0:T(8,128)} custom-call(bf16[8,128,256]{2,1,0:T(8,128)(2,1)S(1)} %get-tuple-element.13.high_ref, bf16[8,128,256]{2,1,0:T(8,128)(2,1)S(1)} %get-tuple-element.14.low_ref, f32[128,256]{1,0:T(8,128)S(1)} %get-tuple-element.15.own_ref, bf16[128,1024]{1,0:T(8,128)(2,1)S(1)} %get-tuple-element.16.second_ref, ...), custom_call_target="tpu_custom_call" | custom-call | tf_op jit(solution)/shard_map/downward/pallas_call | solution.py:298
  (2 shorter events, 0.0 us)
Async XLA Ops:
  0.0 24.8 %copy-start.4 = (s32[1,1,1,8]{3,2,1,0:T(1,128)S(1)}, s32[1,1,1,8]{3,2,1,0:T(1,128)}, u32[]{:S(2)}) copy-start(s32[1,1,1,8]{3,2,1,0:T(1,128)} %param.19) | copy-start | bytes 100
  0.0 24.8 %copy-start.3 = (s32[1,1,1,8]{3,2,1,0:T(1,128)S(1)}, s32[1,1,1,8]{3,2,1,0:T(1,128)}, u32[]{:S(2)}) copy-start(s32[1,1,1,8]{3,2,1,0:T(1,128)} %param.18) | copy-start | bytes 100
  0.0 24.9 %copy-start.2 = (s32[1,1,8,120]{3,2,1,0:T(8,128)S(1)}, s32[1,1,8,120]{3,2,1,0:T(8,128)}, u32[]{:S(2)}) copy-start(s32[1,1,8,120]{3,2,1,0:T(8,128)} %param.17) | copy-start | bytes 11524
  0.0 24.9 %copy-start.1 = (s32[1,1,8,120]{3,2,1,0:T(8,128)S(1)}, s32[1,1,8,120]{3,2,1,0:T(8,128)}, u32[]{:S(2)}) copy-start(s32[1,1,8,120]{3,2,1,0:T(8,128)} %param.16) | copy-start | bytes 11524
  2.9 29.1 %copy-start = (f32[8,64,64]{2,1,0:T(8,128)S(1)}, f32[8,64,64]{2,1,0:T(8,128)}, u32[]{:S(2)}) copy-start(f32[8,64,64]{2,1,0:T(8,128)} %l2l_ref.1) | copy-start | bytes 393220
  2.9 26.9 %all-to-all-start = ((f32[8,32,128]{2,1,0:T(8,128)}), f32[8,32,128]{2,1,0:T(8,128)S(1)}, u32[]{:S(2)}, u32[]{:S(2)}) async-start(f32[8,32,128]{2,1,0:T(8,128)} %get-tuple-element.18), calls=%async_computation | async-start | bytes 262144 | tf_op jit(solution)/shard_map/all_to_all | solution.py:333
  22.2 7.5 %collective-permute-start = (f32[2,64,128]{2,1,0:T(8,128)S(1)}, f32[2,64,128]{2,1,0:T(8,128)S(1)}, u32[]{:S(2)}, u32[]{:S(2)}) collective-permute-start(f32[2,64,128]{2,1,0:T(8,128)S(1)} %get-tuple-element.19), channel_id=1, source_target_pairs={{16,32},{18,34},{20,36},{22,38},{24,40},{26,42},{28,44},{30,46},{3... | collective-permute-start | bytes 196616 | tf_op jit(solution)/shard_map/ppermute | solution.py:327
  22.9 6.8 %collective-permute-start.1 = (f32[2,64,128]{2,1,0:T(8,128)S(1)}, f32[2,64,128]{2,1,0:T(8,128)S(1)}, u32[]{:S(2)}, u32[]{:S(2)}) collective-permute-start(f32[2,64,128]{2,1,0:T(8,128)S(1)} %get-tuple-element.20), channel_id=1, source_target_pairs={{0,16},{1,33},{2,18},{3,35},{4,20},{5,37},{6,22},{7,39},{8,24},{9,... | collective-permute-start | bytes 196616 | tf_op jit(solution)/shard_map/ppermute | solution.py:327
